TPU v7x, 32 devices: a whole 2x2x4 slice. The times are simulated.
32 devices in a mesh: wide: 16 (over z, x, core), narrow: 2 (over y).
Axes of the slice: x: 2, y: 2, z: 4, core: 2. Of those that a mesh axis runs over, the one named last changes fastest.
Arguments:
- small_maps: bfloat16 [256, 16, 16, 256], P('wide', None, None, 'narrow'), may hold values from -6 to 6
- large_maps: bfloat16 [64, 32, 32, 256], P('wide', None, None, 'narrow'), may hold values from -6 to 6
- small_steps: int32 [256], P('wide'), may hold values from 0 to 999
- large_steps: int32 [64], P('wide'), may hold values from 0 to 999
- live_counts: int32 [16, 2], P('wide'), may hold values from 2 to 16, as said below
- small_cotangent: bfloat16 [256, 16, 16, 256], P('wide', None, None, 'narrow'), may hold values from -6 to 6
- large_cotangent: bfloat16 [64, 32, 32, 256], P('wide', None, None, 'narrow'), may hold values from -6 to 6
- first_conv: float32 [256, 2304], P('narrow', 'wide'), may hold values from -0.125 to 0.125
- second_conv: float32 [256, 2304], P('narrow', 'wide'), may hold values from -0.125 to 0.125
- time_dense: float32 [1024, 256], P('wide', 'narrow'), may hold values from -0.1875 to 0.1875
- attn_qkv: float32 [256, 768], P(None, ('wide', 'narrow')), may hold values from -0.375 to 0.375
- attn_proj: float32 [256, 256], P(None, ('wide', 'narrow')), may hold values from -3 to 3
- vectors: float32 [12, 256], P(None, ('wide', 'narrow')), may hold values from -2 to 2
- first_conv_mean: float32 [256, 2304], P('narrow', 'wide')
- first_conv_square: float32 [256, 2304], P('narrow', 'wide')
- second_conv_mean: float32 [256, 2304], P('narrow', 'wide')
- second_conv_square: float32 [256, 2304], P('narrow', 'wide')
- time_dense_mean: float32 [1024, 256], P('wide', 'narrow')
- time_dense_square: float32 [1024, 256], P('wide', 'narrow')
- attn_qkv_mean: float32 [256, 768], P(None, ('wide', 'narrow'))
- attn_qkv_square: float32 [256, 768], P(None, ('wide', 'narrow'))
- attn_proj_mean: float32 [256, 256], P(None, ('wide', 'narrow'))
- attn_proj_square: float32 [256, 256], P(None, ('wide', 'narrow'))
- vectors_mean: float32 [12, 256], P(None, ('wide', 'narrow'))
- vectors_square: float32 [12, 256], P(None, ('wide', 'narrow'))
Outputs:
- small_out: bfloat16 [256, 16, 16, 256], P('wide', None, None, 'narrow')
- large_out: bfloat16 [64, 32, 32, 256], P('wide', None, None, 'narrow')
- small_input_grad: float32 [256, 16, 16, 256], P('wide', None, None, 'narrow')
- large_input_grad: float32 [64, 32, 32, 256], P('wide', None, None, 'narrow')
- first_conv_new: float32 [256, 2304], P('narrow', 'wide')
- first_conv_mean_new: float32 [256, 2304], P('narrow', 'wide')
- first_conv_square_new: float32 [256, 2304], P('narrow', 'wide')
- second_conv_new: float32 [256, 2304], P('narrow', 'wide')
- second_conv_mean_new: float32 [256, 2304], P('narrow', 'wide')
- second_conv_square_new: float32 [256, 2304], P('narrow', 'wide')
- time_dense_new: float32 [1024, 256], P('wide', 'narrow')
- time_dense_mean_new: float32 [1024, 256], P('wide', 'narrow')
- time_dense_square_new: float32 [1024, 256], P('wide', 'narrow')
- attn_qkv_new: float32 [256, 768], P(None, ('wide', 'narrow'))
- attn_qkv_mean_new: float32 [256, 768], P(None, ('wide', 'narrow'))
- attn_qkv_square_new: float32 [256, 768], P(None, ('wide', 'narrow'))
- attn_proj_new: float32 [256, 256], P(None, ('wide', 'narrow'))
- attn_proj_mean_new: float32 [256, 256], P(None, ('wide', 'narrow'))
- attn_proj_square_new: float32 [256, 256], P(None, ('wide', 'narrow'))
- vectors_new: float32 [12, 256], P(None, ('wide', 'narrow'))
- vectors_mean_new: float32 [12, 256], P(None, ('wide', 'narrow'))
- vectors_square_new: float32 [12, 256], P(None, ('wide', 'narrow'))
Inputs may be any that keep to these rules, and one draw needn't show every extreme that they name: `live_counts`: live maps fill the first slots of their index of wide; at some index of wide every slot of both sizes is live.
All inputs are finite; a program needn't handle non-finite values.
Results may differ from a plain program's by a relative error of at most 0.029.
Values may be sent and summed in bfloat16 or wider, within the bound.
No kernel may reach another device: no remote copies, remote signals or barrier semaphores. Data moves between devices by JAX's collectives and lax.ppermute only.
A program may use at most 192 MiB of HBM per device.

v0:
```python
import math

import jax
import jax.numpy as jnp
from jax import lax
from jax.sharding import PartitionSpec as P

GROUPS = 32
STEP_NUMBER = 10


NORM_EPS = 1e-05
ADAM_ONE = 0.9
ADAM_TWO = 0.999
ADAM_EPS = 1e-08
DECAY = 0.01
RATE_CONV = 0.08
RATE_TIME = 0.1
RATE_QKV = 0.2
RATE_PROJ = 1.0
RATE_VECTOR = 1.5
LOG_PERIOD = math.log(10000.0)
PRECISE = lax.Precision.HIGHEST


def cut_along(x, dim, length):
    shape = x.shape
    blocks = x.reshape(*shape[:dim], length, shape[dim] // length, *shape[dim + 1 :])
    return jnp.moveaxis(blocks, dim, 0)


def sent_and_summed(x, axis, dim):
    blocks = cut_along(x, dim, lax.axis_size(axis))
    arrived = lax.all_to_all(blocks, axis, split_axis=0, concat_axis=0, tiled=True)
    return arrived.astype(jnp.float32).sum(axis=0)


def time_features(step_ids, feature_width):
    half_width = feature_width // 2
    frequency = jnp.exp(
        jnp.arange(half_width, dtype=jnp.float32) * (-LOG_PERIOD / (half_width - 1))
    )
    angles = step_ids.astype(jnp.float32)[:, None] * frequency[None, :]
    return jnp.concatenate([jnp.sin(angles), jnp.cos(angles)], axis=1)


def group_norm(inputs, gain, shift, group_size):
    map_count, height, breadth, channel_count = inputs.shape
    grouped = inputs.reshape(map_count, height * breadth, channel_count // group_size, group_size)
    center = jnp.mean(grouped, axis=(1, 3), keepdims=True)
    spread = jnp.mean(jnp.square(grouped - center), axis=(1, 3), keepdims=True)
    inverse = lax.rsqrt(spread + NORM_EPS)
    normal = ((grouped - center) * inverse).reshape(inputs.shape)
    return (normal * gain + shift, normal, inverse)


def group_norm_back(grad_out, normal, inverse, gain, group_size):
    gain_grad = jnp.sum(grad_out * normal, axis=(0, 1, 2))
    shift_grad = jnp.sum(grad_out, axis=(0, 1, 2))
    map_count, height, breadth, channel_count = grad_out.shape
    group_shape = (map_count, height * breadth, channel_count // group_size, group_size)
    scaled = (grad_out * gain).reshape(group_shape)
    grouped = normal.reshape(group_shape)
    mean_grad = jnp.mean(scaled, axis=(1, 3), keepdims=True)
    mean_cross = jnp.mean(scaled * grouped, axis=(1, 3), keepdims=True)
    input_grad = (inverse * (scaled - mean_grad - grouped * mean_cross)).reshape(grad_out.shape)
    return (input_grad, gain_grad, shift_grad)


def silu_grad(activation_in):
    logistic = jax.nn.sigmoid(activation_in)
    return logistic * (1.0 + activation_in * (1.0 - logistic))


def conv_apply(inputs, kernel):
    return lax.conv_general_dilated(
        inputs,
        kernel,
        (1, 1),
        "SAME",
        dimension_numbers=("NHWC", "HWIO", "NHWC"),
        preferred_element_type=jnp.float32,
    )


def conv_input_grad(grads, kernel):
    return conv_apply(grads, jnp.transpose(kernel[::-1, ::-1], (0, 1, 3, 2)))


def conv_weight_grad(inputs, grads):
    height = inputs.shape[1]
    breadth = inputs.shape[2]
    padded = jnp.pad(inputs, ((0, 0), (1, 1), (1, 1), (0, 0)))
    tap_terms = []
    for tap_row in range(3):
        for tap_col in range(3):
            window = padded[:, tap_row : tap_row + height, tap_col : tap_col + breadth, :]
            tap_terms.append(
                jnp.einsum("nhwc,nhwd->cd", window, grads, preferred_element_type=jnp.float32)
            )
    stacked = jnp.stack(tap_terms, axis=1)
    return stacked.reshape(stacked.shape[0], -1)


def conv_layer(activated, kernel_part):
    return (
        lax.psum_scatter(
            conv_apply(activated[0], kernel_part).astype(jnp.bfloat16),
            "narrow",
            scatter_dimension=3,
            tiled=True,
        ).astype(jnp.float32),
        lax.psum_scatter(
            conv_apply(activated[1], kernel_part).astype(jnp.bfloat16),
            "narrow",
            scatter_dimension=3,
            tiled=True,
        ).astype(jnp.float32),
    )


def conv_grads(small_grad, large_grad):
    return (
        lax.all_gather(small_grad, "narrow", axis=3, tiled=True),
        lax.all_gather(large_grad, "narrow", axis=3, tiled=True),
    )


def flat_rows(block):
    return block.reshape(block.shape[0], -1, block.shape[3])


def attend(queries, key_rows, values, score_scale):
    scores = (
        jnp.einsum("nqc,nkc->nqk", queries, key_rows, preferred_element_type=jnp.float32)
        * score_scale
    )
    row_max = jnp.max(scores, axis=2, keepdims=True)
    exponent = jnp.exp(scores - row_max)
    row_total = jnp.sum(exponent, axis=2, keepdims=True)
    softmax_probs = (exponent / row_total).astype(jnp.bfloat16)
    mixture = jnp.einsum("nqk,nkc->nqc", softmax_probs, values, preferred_element_type=jnp.float32)
    return (mixture.astype(jnp.bfloat16), row_max + jnp.log(row_total))


def attend_back(queries, key_rows, values, logsum, grad_mixture, score_scale):
    scores = (
        jnp.einsum("nqc,nkc->nqk", queries, key_rows, preferred_element_type=jnp.float32)
        * score_scale
    )
    softmax_probs = jnp.exp(scores - logsum)
    grad_probs = jnp.einsum(
        "nqc,nkc->nqk", grad_mixture, values, preferred_element_type=jnp.float32
    )
    grad_values = jnp.einsum(
        "nqk,nqc->nkc",
        softmax_probs.astype(jnp.bfloat16),
        grad_mixture,
        preferred_element_type=jnp.float32,
    )
    inner = jnp.sum(softmax_probs * grad_probs, axis=2, keepdims=True)
    grad_scores = (softmax_probs * (grad_probs - inner)).astype(jnp.bfloat16)
    grad_queries = jnp.einsum(
        "nqk,nkc->nqc", grad_scores, key_rows, preferred_element_type=jnp.float32
    )
    grad_keys = jnp.einsum("nqk,nqc->nkc", grad_scores, queries, preferred_element_type=jnp.float32)
    return ((grad_queries * score_scale).astype(jnp.bfloat16), grad_keys * score_scale, grad_values)


def adam_step(weight, grad, mean, square, rate, decay):
    mean_new = ADAM_ONE * mean + (1.0 - ADAM_ONE) * grad
    square_new = ADAM_TWO * square + (1.0 - ADAM_TWO) * grad * grad
    first_fix = mean_new / (1.0 - ADAM_ONE**STEP_NUMBER)
    second_fix = square_new / (1.0 - ADAM_TWO**STEP_NUMBER)
    weight_new = weight - rate * (first_fix / (jnp.sqrt(second_fix) + ADAM_EPS) + decay * weight)
    return (weight_new, mean_new, square_new)


def per_device(
    small_maps,
    large_maps,
    small_steps,
    large_steps,
    live_counts,
    small_cotangent,
    large_cotangent,
    first_conv,
    second_conv,
    time_dense,
    attn_qkv,
    attn_proj,
    vectors,
    first_conv_mean,
    first_conv_square,
    second_conv_mean,
    second_conv_square,
    time_dense_mean,
    time_dense_square,
    attn_qkv_mean,
    attn_qkv_square,
    attn_proj_mean,
    attn_proj_square,
    vectors_mean,
    vectors_square,
):
    channel_count = attn_qkv.shape[0]
    local_width = first_conv.shape[0]
    group_size = channel_count // GROUPS
    offset = lax.axis_index("narrow") * local_width
    score_scale = 1.0 / math.sqrt(channel_count)
    conv_one, conv_two, time_weight = (
        lax.all_gather(first_conv.astype(jnp.bfloat16), "wide", axis=1, tiled=True),
        lax.all_gather(second_conv.astype(jnp.bfloat16), "wide", axis=1, tiled=True),
        lax.all_gather(time_dense.astype(jnp.bfloat16), "wide", axis=0, tiled=True),
    )
    qkv_weight, proj_weight, vector_low = (
        lax.all_gather(attn_qkv.astype(jnp.bfloat16), ("wide", "narrow"), axis=1, tiled=True),
        lax.all_gather(attn_proj.astype(jnp.bfloat16), ("wide", "narrow"), axis=1, tiled=True),
        lax.all_gather(vectors.astype(jnp.bfloat16), ("wide", "narrow"), axis=1, tiled=True),
    )
    vector_all = vector_low.astype(jnp.float32)
    vector_own = lax.dynamic_slice_in_dim(vector_all, offset, local_width, 1)
    kernel_one = conv_one.reshape(local_width, 3, 3, channel_count).transpose(1, 2, 0, 3)
    kernel_two = conv_two.reshape(local_width, 3, 3, channel_count).transpose(1, 2, 0, 3)
    qkv_bias = jnp.concatenate(
        [vector_all[9], jnp.zeros((channel_count,), jnp.float32), vector_all[10]]
    )
    feature_width = time_weight.shape[0]
    map_list = [small_maps, large_maps]
    live_list = [
        (jnp.arange(small_maps.shape[0]) < live_counts[0, 0]).astype(jnp.float32),
        (jnp.arange(large_maps.shape[0]) < live_counts[0, 1]).astype(jnp.float32),
    ]
    cotangent_list = [small_cotangent, large_cotangent]
    time_feats = [
        jax.nn.silu(time_features(small_steps, feature_width)).astype(jnp.bfloat16),
        jax.nn.silu(time_features(large_steps, feature_width)).astype(jnp.bfloat16),
    ]
    first_norm = []
    first_act = []
    for group_index in range(2):
        normed, normal, inverse = group_norm(
            map_list[group_index].astype(jnp.float32), vector_own[0], vector_own[1], group_size
        )
        first_norm.append((normed, normal, inverse))
        first_act.append(jax.nn.silu(normed).astype(jnp.bfloat16))
    summed = conv_layer(first_act, kernel_one)
    second_norm = []
    second_act = []
    for group_index in range(2):
        time_add = (
            jnp.dot(time_feats[group_index], time_weight, preferred_element_type=jnp.float32)
            + vector_own[7]
        )
        hidden = summed[group_index] + vector_own[6] + time_add[:, None, None, :]
        normed, normal, inverse = group_norm(hidden, vector_own[2], vector_own[3], group_size)
        second_norm.append((normed, normal, inverse))
        second_act.append(jax.nn.silu(normed).astype(jnp.bfloat16))
    summed = conv_layer(second_act, kernel_two)
    block_sums = []
    third_norm = []
    sent_norm = []
    sent_grad = []
    for group_index in range(2):
        block_sum = map_list[group_index].astype(jnp.float32) + summed[group_index] + vector_own[8]
        normed, normal, inverse = group_norm(block_sum, vector_own[4], vector_own[5], group_size)
        block_sums.append(block_sum)
        third_norm.append((normal, inverse))
        sent_norm.append(normed.astype(jnp.bfloat16))
        masked = (
            cotangent_list[group_index].astype(jnp.float32)
            * live_list[group_index][:, None, None, None]
        )
        sent_grad.append(masked.astype(jnp.bfloat16))
    norm_small, norm_large, grad_small, grad_large = (
        lax.all_to_all(sent_norm[0], "narrow", split_axis=1, concat_axis=3, tiled=True),
        lax.all_to_all(sent_norm[1], "narrow", split_axis=1, concat_axis=3, tiled=True),
        lax.all_to_all(sent_grad[0], "narrow", split_axis=1, concat_axis=3, tiled=True),
        lax.all_to_all(sent_grad[1], "narrow", split_axis=1, concat_axis=3, tiled=True),
    )
    shape_list = [norm_small.shape, norm_large.shape]
    attn_in = [flat_rows(norm_small), flat_rows(norm_large)]
    attn_grad = [flat_rows(grad_small), flat_rows(grad_large)]
    query_list = []
    own_pairs = []
    for group_index in range(2):
        projected = (
            jnp.einsum(
                "npc,cd->npd", attn_in[group_index], qkv_weight, preferred_element_type=jnp.float32
            )
            + qkv_bias
        )
        projected = projected.astype(jnp.bfloat16)
        query_list.append(projected[..., :channel_count])
        own_pairs.append(projected[..., channel_count:])
    pair_small, pair_large = (
        lax.all_gather(own_pairs[0], "narrow", axis=1, tiled=True),
        lax.all_gather(own_pairs[1], "narrow", axis=1, tiled=True),
    )
    pair_list = [pair_small, pair_large]
    mixtures = []
    logsums = []
    branches = []
    for group_index in range(2):
        key_rows = pair_list[group_index][..., :channel_count]
        values = pair_list[group_index][..., channel_count:]
        mixture, logsum = attend(query_list[group_index], key_rows, values, score_scale)
        mixtures.append(mixture)
        logsums.append(logsum)
        branch = (
            jnp.einsum("npc,cd->npd", mixture, proj_weight, preferred_element_type=jnp.float32)
            + vector_all[11]
        )
        branches.append(branch.astype(jnp.bfloat16).reshape(shape_list[group_index]))
    back_small, back_large = (
        lax.all_to_all(branches[0], "narrow", split_axis=3, concat_axis=1, tiled=True),
        lax.all_to_all(branches[1], "narrow", split_axis=3, concat_axis=1, tiled=True),
    )
    back_list = [back_small, back_large]
    outputs = []
    for group_index in range(2):
        result = (block_sums[group_index] + back_list[group_index].astype(jnp.float32)) * live_list[
            group_index
        ][:, None, None, None]
        outputs.append(result.astype(jnp.bfloat16))
    proj_grad = jnp.zeros((channel_count, channel_count), jnp.float32)
    proj_bias_grad = jnp.zeros((channel_count,), jnp.float32)
    query_grads = []
    pair_parts = []
    for group_index in range(2):
        grad_rows = attn_grad[group_index]
        proj_grad = proj_grad + jnp.einsum(
            "npc,npd->cd", mixtures[group_index], grad_rows, preferred_element_type=jnp.float32
        )
        proj_bias_grad = proj_bias_grad + jnp.sum(grad_rows, axis=(0, 1), dtype=jnp.float32)
        grad_mixture = jnp.einsum(
            "npd,cd->npc", grad_rows, proj_weight, preferred_element_type=jnp.float32
        ).astype(jnp.bfloat16)
        key_rows = pair_list[group_index][..., :channel_count]
        values = pair_list[group_index][..., channel_count:]
        grad_queries, grad_keys, grad_values = attend_back(
            query_list[group_index],
            key_rows,
            values,
            logsums[group_index],
            grad_mixture,
            score_scale,
        )
        query_grads.append(grad_queries)
        pair_parts.append(jnp.concatenate([grad_keys, grad_values], axis=2))
    pair_sum_small, pair_sum_large = (
        lax.psum_scatter(
            pair_parts[0].astype(jnp.bfloat16), "narrow", scatter_dimension=1, tiled=True
        ).astype(jnp.float32),
        lax.psum_scatter(
            pair_parts[1].astype(jnp.bfloat16), "narrow", scatter_dimension=1, tiled=True
        ).astype(jnp.float32),
    )
    pair_sums = [pair_sum_small, pair_sum_large]
    qkv_grad = jnp.zeros((channel_count, 3 * channel_count), jnp.float32)
    qkv_bias_grad = jnp.zeros((3 * channel_count,), jnp.float32)
    norm_grads = []
    for group_index in range(2):
        joined = jnp.concatenate(
            [query_grads[group_index], pair_sums[group_index].astype(jnp.bfloat16)], axis=2
        )
        qkv_grad = qkv_grad + jnp.einsum(
            "npc,npd->cd", attn_in[group_index], joined, preferred_element_type=jnp.float32
        )
        qkv_bias_grad = qkv_bias_grad + jnp.sum(joined, axis=(0, 1), dtype=jnp.float32)
        norm_grad = jnp.einsum(
            "npd,cd->npc", joined, qkv_weight, preferred_element_type=jnp.float32
        )
        norm_grads.append(norm_grad.astype(jnp.bfloat16).reshape(shape_list[group_index]))
    chan_small, chan_large = (
        lax.all_to_all(norm_grads[0], "narrow", split_axis=3, concat_axis=1, tiled=True),
        lax.all_to_all(norm_grads[1], "narrow", split_axis=3, concat_axis=1, tiled=True),
    )
    chan_grads = [chan_small, chan_large]
    chan_rows = [jnp.zeros((local_width,), jnp.float32) for row_index in range(9)]
    block_grads = []
    rounded = []
    for group_index in range(2):
        normal, inverse = third_norm[group_index]
        input_part, gain_grad, shift_grad = group_norm_back(
            chan_grads[group_index].astype(jnp.float32), normal, inverse, vector_own[4], group_size
        )
        chan_rows[4] = chan_rows[4] + gain_grad
        chan_rows[5] = chan_rows[5] + shift_grad
        block_grad = sent_grad[group_index].astype(jnp.float32) + input_part
        block_grads.append(block_grad)
        block_low = block_grad.astype(jnp.bfloat16)
        chan_rows[8] = chan_rows[8] + jnp.sum(block_low, axis=(0, 1, 2), dtype=jnp.float32)
        rounded.append(block_low)
    full_grads = conv_grads(rounded[0], rounded[1])
    conv_two_grad = jnp.zeros((local_width, 9 * channel_count), jnp.float32)
    time_grad = jnp.zeros((feature_width, local_width), jnp.float32)
    rounded = []
    for group_index in range(2):
        conv_two_grad = conv_two_grad + conv_weight_grad(
            second_act[group_index], full_grads[group_index]
        )
        act_grad = conv_input_grad(full_grads[group_index], kernel_two)
        normed, normal, inverse = second_norm[group_index]
        hidden_grad, gain_grad, shift_grad = group_norm_back(
            act_grad * silu_grad(normed), normal, inverse, vector_own[2], group_size
        )
        chan_rows[2] = chan_rows[2] + gain_grad
        chan_rows[3] = chan_rows[3] + shift_grad
        hidden_low = hidden_grad.astype(jnp.bfloat16)
        chan_rows[6] = chan_rows[6] + jnp.sum(hidden_low, axis=(0, 1, 2), dtype=jnp.float32)
        time_rows = jnp.sum(hidden_low, axis=(1, 2), dtype=jnp.float32)
        chan_rows[7] = chan_rows[7] + jnp.sum(time_rows, axis=0)
        time_grad = time_grad + jnp.dot(
            time_feats[group_index].astype(jnp.float32).T, time_rows, precision=PRECISE
        )
        rounded.append(hidden_low)
    full_grads = conv_grads(rounded[0], rounded[1])
    conv_one_grad = jnp.zeros((local_width, 9 * channel_count), jnp.float32)
    input_grads = []
    for group_index in range(2):
        conv_one_grad = conv_one_grad + conv_weight_grad(
            first_act[group_index], full_grads[group_index]
        )
        act_grad = conv_input_grad(full_grads[group_index], kernel_one)
        normed, normal, inverse = first_norm[group_index]
        input_part, gain_grad, shift_grad = group_norm_back(
            act_grad * silu_grad(normed), normal, inverse, vector_own[0], group_size
        )
        chan_rows[0] = chan_rows[0] + gain_grad
        chan_rows[1] = chan_rows[1] + shift_grad
        input_grads.append(block_grads[group_index] + input_part)
    chan_block = jnp.stack(chan_rows, axis=0)
    chan_full = lax.dynamic_update_slice_in_dim(
        jnp.zeros((9, channel_count), jnp.float32), chan_block, offset, 1
    )
    attn_rows = jnp.stack(
        [qkv_bias_grad[:channel_count], qkv_bias_grad[2 * channel_count :], proj_bias_grad], axis=0
    )
    vector_grad = jnp.concatenate([chan_full, attn_rows], axis=0)
    conv_one_sum, conv_two_sum, time_sum = (
        sent_and_summed(conv_one_grad.astype(jnp.bfloat16), "wide", 1),
        sent_and_summed(conv_two_grad.astype(jnp.bfloat16), "wide", 1),
        sent_and_summed(time_grad.astype(jnp.bfloat16), "wide", 0),
    )
    qkv_sum, proj_sum, vector_sum = (
        lax.psum_scatter(qkv_grad, ("wide", "narrow"), scatter_dimension=1, tiled=True),
        lax.psum_scatter(proj_grad, ("wide", "narrow"), scatter_dimension=1, tiled=True),
        lax.psum_scatter(vector_grad, ("wide", "narrow"), scatter_dimension=1, tiled=True),
    )
    conv_one_new = adam_step(
        first_conv, conv_one_sum, first_conv_mean, first_conv_square, RATE_CONV, DECAY
    )
    conv_two_new = adam_step(
        second_conv, conv_two_sum, second_conv_mean, second_conv_square, RATE_CONV, DECAY
    )
    time_new = adam_step(time_dense, time_sum, time_dense_mean, time_dense_square, RATE_TIME, DECAY)
    qkv_new = adam_step(attn_qkv, qkv_sum, attn_qkv_mean, attn_qkv_square, RATE_QKV, DECAY)
    proj_new = adam_step(attn_proj, proj_sum, attn_proj_mean, attn_proj_square, RATE_PROJ, DECAY)
    vector_new = adam_step(vectors, vector_sum, vectors_mean, vectors_square, RATE_VECTOR, 0.0)
    return (
        outputs[0],
        outputs[1],
        input_grads[0],
        input_grads[1],
        conv_one_new[0],
        conv_one_new[1],
        conv_one_new[2],
        conv_two_new[0],
        conv_two_new[1],
        conv_two_new[2],
        time_new[0],
        time_new[1],
        time_new[2],
        qkv_new[0],
        qkv_new[1],
        qkv_new[2],
        proj_new[0],
        proj_new[1],
        proj_new[2],
        vector_new[0],
        vector_new[1],
        vector_new[2],
    )


def solution(mesh):
    return jax.shard_map(
        per_device,
        mesh=mesh,
        in_specs=(
            P("wide", None, None, "narrow"),
            P("wide", None, None, "narrow"),
            P("wide"),
            P("wide"),
            P("wide", None),
            P("wide", None, None, "narrow"),
            P("wide", None, None, "narrow"),
            P("narrow", "wide"),
            P("narrow", "wide"),
            P("wide", "narrow"),
            P(None, ("wide", "narrow")),
            P(None, ("wide", "narrow")),
            P(None, ("wide", "narrow")),
            P("narrow", "wide"),
            P("narrow", "wide"),
            P("narrow", "wide"),
            P("narrow", "wide"),
            P("wide", "narrow"),
            P("wide", "narrow"),
            P(None, ("wide", "narrow")),
            P(None, ("wide", "narrow")),
            P(None, ("wide", "narrow")),
            P(None, ("wide", "narrow")),
            P(None, ("wide", "narrow")),
            P(None, ("wide", "narrow")),
        ),
        out_specs=(
            P("wide", None, None, "narrow"),
            P("wide", None, None, "narrow"),
            P("wide", None, None, "narrow"),
            P("wide", None, None, "narrow"),
            P("narrow", "wide"),
            P("narrow", "wide"),
            P("narrow", "wide"),
            P("narrow", "wide"),
            P("narrow", "wide"),
            P("narrow", "wide"),
            P("wide", "narrow"),
            P("wide", "narrow"),
            P("wide", "narrow"),
            P(None, ("wide", "narrow")),
            P(None, ("wide", "narrow")),
            P(None, ("wide", "narrow")),
            P(None, ("wide", "narrow")),
            P(None, ("wide", "narrow")),
            P(None, ("wide", "narrow")),
            P(None, ("wide", "narrow")),
            P(None, ("wide", "narrow")),
            P(None, ("wide", "narrow")),
        ),
        check_vma=False,
    )
```

profile of v0, /device:TPU:0, one launch (start us, length us, event | category | flops | bytes accessed | tf_op | source)
XLA Modules:
  0.0 1429.3 jit_solution(2245085704645257741)
XLA Ops:
  11.7 70.0 %all_gather.36 = bf16[12,256]{0,1:T(8,128)(2,1)S(1)} all-gather(bf16[12,8]{0,1:T(8,128)(2,1)S(1)} %convert_element_type.326), channel_id=1, replica_groups=mesh['wide'=16,'narrow'=2] {'wide','narrow'}, dimensions={1}, use_global_device_ids=true | all-gather | bytes 6336 | tf_op jit(solution)/shard_map/all_gather | solution.py:219
  81.7 20.4 %all_gather.37 = bf16[128,2304]{0,1:T(8,128)(2,1)} all-gather(bf16[128,144]{0,1:T(8,128)(2,1)S(1)} %convert_element_type.329), channel_id=1, replica_groups=mesh['wide'=16,'narrow'=2] {'wide'}, dimensions={1}, use_global_device_ids=true | all-gather | bytes 626688 | tf_op jit(solution)/shard_map/all_gather | solution.py:212
  111.5 13.7 copy.504
  125.3 11.7 reshape.647
  146.0 23.4 %copy.500 = bf16[16,16,16,256]{0,2,1,3:T(8,128)(2,1)} copy(bf16[16,16,16,256]{3,0,2,1:T(8,128)(2,1)} %convolution_convert_fusion.2) | data formatting | bytes 4194304
  169.5 29.7 %reshape.643 = bf16[256,4096]{1,0:T(8,128)(2,1)} reshape(bf16[256,16,16,16]{3,2,1,0:T(8,128)(2,1)} %bitcast.673) | data formatting | bytes 4194304
  200.1 19.7 %all_gather.38 = bf16[1024,128]{1,0:T(8,128)(2,1)S(1)} all-gather(bf16[64,128]{1,0:T(8,128)(2,1)S(1)} %convert_element_type.334), channel_id=1, replica_groups=mesh['wide'=16,'narrow'=2] {'wide'}, dimensions={0}, use_global_device_ids=true | all-gather | bytes 278528 | tf_op jit(solution)/shard_map/all_gather | solution.py:214
  220.2 20.6 %all_gather.39 = bf16[128,2304]{0,1:T(8,128)(2,1)} all-gather(bf16[128,144]{0,1:T(8,128)(2,1)S(1)} %convert_element_type.336), channel_id=1, replica_groups=mesh['wide'=16,'narrow'=2] {'wide'}, dimensions={1}, use_global_device_ids=true | all-gather | bytes 626688 | tf_op jit(solution)/shard_map/all_gather | solution.py:213
  240.8 5.7 reshape.648
  246.5 6.0 copy.505
  273.1 15.1 %copy.506 = bf16[4,32,32,256]{2,0,1,3:T(4,128)(2,1)} copy(bf16[4,32,32,256]{3,1,2,0:T(8,128)(2,1)} %slice_bitcast_fusion) | data formatting | bytes 4194304
  288.2 11.7 reshape.649
  301.1 9.1 reshape.644
  310.2 10.1 copy.501
  327.6 23.4 %copy.502 = bf16[16,16,16,256]{0,2,1,3:T(8,128)(2,1)} copy(bf16[16,16,16,256]{3,0,2,1:T(8,128)(2,1)} %convolution_convert_fusion.1) | data formatting | bytes 4194304
  351.0 29.7 %reshape.645 = bf16[256,4096]{1,0:T(8,128)(2,1)} reshape(bf16[256,16,16,16]{3,2,1,0:T(8,128)(2,1)} %bitcast.674) | data formatting | bytes 4194304
  380.8 5.7 reshape.650
  386.5 5.9 copy.507
  401.5 81.0 %all_gather.40 = bf16[256,768]{0,1:T(8,128)(2,1)S(1)} all-gather(bf16[256,24]{0,1:T(8,128)(2,1)S(1)} %convert_element_type.340), channel_id=1, replica_groups=mesh['wide'=16,'narrow'=2] {'wide','narrow'}, dimensions={1}, use_global_device_ids=true | all-gather | bytes 405504 | tf_op jit(solution)/shard_map/all_gather | solution.py:217
  490.6 9.2 reshape.646
  499.9 10.0 copy.503
  521.6 27.4 %all_to_all.111 = bf16[16,16,16,128]{3,0,2,1:T(8,128)(2,1)S(1)} all-to-all(bf16[16,16,16,128]{3,0,2,1:T(8,128)(2,1)S(1)} %add_convert_fusion.5), channel_id=1, replica_groups=mesh['wide'=16,'narrow'=2] {'narrow'}, dimensions={1} | all-to-all | bytes 2097152 | tf_op jit(solution)/shard_map/all_to_all | solution.py:276
  571.7 21.4 %all-to-all-done.4 = bf16[16,16,16,128]{3,0,2,1:T(8,128)(2,1)} async-done(((bf16[16,16,16,128]{3,0,2,1:T(8,128)(2,1)}), bf16[16,16,16,128]{3,0,2,1:T(8,128)(2,1)}, u32[]{:S(2)}, u32[]{:S(2)}) %all-to-all-start.4) | async-done | bytes 1048608 | tf_op jit(solution)/shard_map/all_to_all | solution.py:278
  603.6 18.5 %all-to-all-done.6 = bf16[4,32,32,128]{3,2,0,1:T(8,128)(2,1)} async-done(((bf16[4,32,32,128]{3,2,0,1:T(8,128)(2,1)}), bf16[4,32,32,128]{3,2,0,1:T(8,128)(2,1)}, u32[]{:S(2)}, u32[]{:S(2)}) %all-to-all-start.6) | async-done | bytes 1048608 | tf_op jit(solution)/shard_map/all_to_all | solution.py:279
  647.3 129.4 %reduce-scatter.23.cloned.1.call-done = f32[256,8]{0,1:T(8,128)} async-done(((f32[256,256]{0,1:T(8,128)}), f32[256,8]{0,1:T(8,128)}) %reduce-scatter.23.cloned.1.call-update) | async-done | bytes 8208 | tf_op jit(solution)/shard_map/reduce_scatter | solution.py:448
  778.1 64.3 %all_gather.42 = bf16[256,256]{0,1:T(8,128)(2,1)S(1)} all-gather(bf16[256,8]{0,1:T(8,128)(2,1)S(1)} %get-tuple-element.204), channel_id=1, replica_groups=mesh['wide'=16,'narrow'=2] {'wide','narrow'}, dimensions={1}, use_global_device_ids=true | all-gather | bytes 135168 | tf_op jit(solution)/shard_map/all_gather | solution.py:218
  853.4 8.0 copy.508
  861.4 8.4 copy.519
  872.0 6.5 multiply_reduce_fusion
  893.4 28.8 %reduce-scatter.33.cloned.1.call-done = bf16[128,8192]{1,0:T(8,128)(2,1)} async-done(((bf16[256,8192]{1,0:T(8,128)(2,1)}), bf16[128,8192]{1,0:T(8,128)(2,1)}) %reduce-scatter.33.cloned.1.call-update) | async-done | bytes 2097168
  928.0 12.6 copy.409
  940.6 12.1 reshape.669
  952.7 4.6 all-to-all-start.5
  959.2 5.2 multiply_convert_fusion.4
  964.4 18.9 %all-to-all-done.5 = bf16[2,2,131072]{2,1,0:T(2,128)(2,1)} async-done(((bf16[2,2,131072]{2,1,0:T(2,128)(2,1)}), bf16[2,2,131072]{2,1,0:T(2,128)(2,1)}, u32[]{:S(2)}, u32[]{:S(2)}) %all-to-all-start.5) | async-done | bytes 1048608 | tf_op jit(solution)/shard_map/all_to_all | solution.py:376
  983.2 8.8 reshape.670
  992.1 11.3 copy.499
  1010.8 5.8 convert_reduce_fusion.13
  1019.7 6.6 copy.433
  1026.3 6.7 reshape.671
  1041.8 6.5 copy.402
  1048.3 6.5 reshape.667
  1054.8 6.2 all-to-all-done.7
  1060.9 4.5 all-to-all-start.3
  1069.1 6.1 copy.434
  1084.8 12.0 copy.389
  1096.8 11.7 reshape.665
  1118.5 4.6 reshape.668
  1123.1 7.2 copy.403
  1130.2 7.9 reshape.666
  1138.1 9.7 copy.390
  1159.3 5.5 convert_reduce_fusion.2
  1167.0 9.8 multiply_reduce_fusion.3
  1181.1 9.4 fusion.116
  1204.7 5.6 all-to-all-start.10
  1223.6 6.1 all-to-all-start.9
  1230.8 29.3 %reduce-scatter.21.cloned.1.call-done = f32[256,24]{0,1:T(8,128)} async-done(((f32[256,768]{0,1:T(8,128)}), f32[256,24]{0,1:T(8,128)}) %reduce-scatter.21.cloned.1.call-update) | async-done | bytes 24592 | tf_op jit(solution)/shard_map/reduce_scatter | solution.py:447
  1264.2 30.3 %all-gather.13.cloned.1.call-done = bf16[16,16,16,256]{3,0,2,1:T(8,128)(2,1)} async-done(((bf16[16,16,16,128]{3,0,2,1:T(8,128)(2,1)}), bf16[16,16,16,256]{3,0,2,1:T(8,128)(2,1)}) %all-gather.13.cloned.1.call-update) | async-done | bytes 2097168 | tf_op jit(solution)/shard_map/all_gather | solution.py:124
  1294.5 11.1 fusion.63
  1316.5 12.5 all-gather.17.cloned.1.call-done
  1338.6 5.7 all-to-all-start.8
  1346.9 9.4 fusion.119
  1364.8 6.5 fusion.62
  1379.3 40.7 %all-reduce.4 = f32[12,256]{0,1:T(8,128)S(1)} all-reduce(f32[12,256]{0,1:T(8,128)S(1)} %copy.449), channel_id=10, replica_groups=mesh['wide'=16,'narrow'=2] {'wide','narrow'}, use_global_device_ids=true, to_apply=%region_89.90.clone | all-reduce | flops 3072 | bytes 24576
  (718 shorter events, 310.5 us)
Async XLA Ops:
  7.2 95.9 %copy-start.11 = (bf16[4,32,32,128]{3,2,1,0:T(8,128)(2,1)S(1)}, bf16[4,32,32,128]{3,2,1,0:T(8,128)(2,1)}, u32[]{:S(2)}) copy-start(bf16[4,32,32,128]{3,2,1,0:T(8,128)(2,1)} %param.26) | copy-start | bytes 3145732
  7.2 233.6 %reduce-scatter.29.cloned.1.call-start = ((), (), s32[]{:S(2)}) async-start(), calls=%async_computation.30 | async-start | bytes 3145728
  9.8 94.1 %copy-start.98 = (f32[4,128]{1,0:T(4,128)}, f32[4,128]{1,0:T(4,128)S(1)}, u32[]{:S(2)}) copy-start(f32[4,128]{1,0:T(4,128)S(1)} %sub.323) | copy-start | bytes 6148
  11.7 92.9 %copy-start.105 = (f32[4,128]{1,0:T(4,128)}, f32[4,128]{1,0:T(4,128)S(1)}, u32[]{:S(2)}) copy-start(f32[4,128]{1,0:T(4,128)S(1)} %mul.757) | copy-start | bytes 6148
  103.1 116.9 %copy-start.159 = (f32[128]{0:T(128)}, f32[128]{0:T(128)S(1)}, u32[]{:S(2)}) copy-start(f32[128]{0:T(128)S(1)} %get-tuple-element.166) | copy-start | bytes 1540
  103.1 218.4 %copy-start.102 = (f32[128]{0:T(128)}, f32[128]{0:T(128)S(1)}, u32[]{:S(2)}) copy-start(f32[128]{0:T(128)S(1)} %get-tuple-element.161) | copy-start | bytes 1540
  103.1 411.8 %copy-start.100 = (f32[128]{0:T(128)}, f32[128]{0:T(128)S(1)}, u32[]{:S(2)}) copy-start(f32[128]{0:T(128)S(1)} %get-tuple-element.163) | copy-start | bytes 1540
  137.0 164.0 %reduce-scatter.25.cloned.1.call-start = ((), (), s32[]{:S(2)}) async-start(), calls=%async_computation.28 | async-start | bytes 3145728
  199.2 181.6 %reduce-scatter.31.cloned.1.call-start = ((), (), s32[]{:S(2)}) async-start(), calls=%async_computation.31 | async-start | bytes 3145728
  220.2 42.3 %copy-start.84 = (f32[4,128]{1,0:T(4,128)}, f32[4,128]{1,0:T(4,128)S(1)}, u32[]{:S(2)}) copy-start(f32[4,128]{1,0:T(4,128)S(1)} %convolution_add_fusion.2) | copy-start | bytes 6148
  300.0 190.6 %reduce-scatter.27.cloned.1.call-start = ((), (), s32[]{:S(2)}) async-start(), calls=%async_computation.29 | async-start | bytes 3145728
  397.0 85.5 %all-to-all-start.2 = ((bf16[4,32,32,128]{3,2,0,1:T(8,128)(2,1)}), bf16[4,32,32,128]{3,2,0,1:T(8,128)(2,1)S(1)}, u32[]{:S(2)}, u32[]{:S(2)}) async-start(bf16[4,32,32,128]{3,2,0,1:T(8,128)(2,1)} %add_convert_fusion.3), calls=%async_computation.2 | async-start | bytes 2097152 | tf_op jit(solution)/shard_map/all_to_all | solution.py:277
  400.6 227.3 %all-gather.9.cloned.1.call-start = ((), (), s32[]{:S(2)}) async-start(), calls=%async_computation.20 | async-start | bytes 6291456 | tf_op jit(solution)/shard_map/all_gather | solution.py:298
  401.5 84.8 %copy-start.150 = (f32[768]{0:T(1024)}, f32[768]{0:T(1024)S(1)}, u32[]{:S(2)}) copy-start(f32[768]{0:T(1024)S(1)} %pad_maximum_fusion.11) | copy-start | bytes 9220
  482.5 71.1 %copy-start.62 = (bf16[256,768]{0,1:T(8,128)(2,1)}, bf16[256,768]{0,1:T(8,128)(2,1)S(1)}, u32[]{:S(2)}) copy-start(bf16[256,768]{0,1:T(8,128)(2,1)S(1)} %all_gather.40) | copy-start | bytes 1179652
  490.5 149.6 %all-gather.7.cloned.1.call-start = ((), (), s32[]{:S(2)}) async-start(), calls=%async_computation.19 | async-start | bytes 6291456 | tf_op jit(solution)/shard_map/all_gather | solution.py:297
  509.9 500.9 %copy-start.25 = (bf16[16,16,16,128]{3,0,2,1:T(8,128)(2,1)}, bf16[16,16,16,128]{3,0,2,1:T(8,128)(2,1)S(1)}, u32[]{:S(2)}) copy-start(bf16[16,16,16,128]{3,0,2,1:T(8,128)(2,1)S(1)} %copy.503) | copy-start | bytes 3145732
  560.9 449.9 %copy-start.145 = (f32[16]{0:T(128)}, f32[16]{0:T(128)S(1)}, u32[]{:S(2)}) copy-start(f32[16]{0:T(128)S(1)} %compare_convert_fusion.1) | copy-start | bytes 196
  563.9 29.2 %all-to-all-start.4 = ((bf16[16,16,16,128]{3,0,2,1:T(8,128)(2,1)}), bf16[16,16,16,128]{3,0,2,1:T(8,128)(2,1)}, u32[]{:S(2)}, u32[]{:S(2)}) async-start(bf16[16,16,16,128]{3,0,2,1:T(8,128)(2,1)} %multiply_convert_fusion.9), calls=%async_computation.4 | async-start | bytes 2097152 | tf_op jit(solution)/shard_map/all_to_all | solution.py:278
  569.1 509.7 %copy-start.143 = (f32[4]{0:T(128)}, f32[4]{0:T(128)S(1)}, u32[]{:S(2)}) copy-start(f32[4]{0:T(128)S(1)} %compare_convert_fusion) | copy-start | bytes 52
  593.2 28.9 %all-to-all-start.6 = ((bf16[4,32,32,128]{3,2,0,1:T(8,128)(2,1)}), bf16[4,32,32,128]{3,2,0,1:T(8,128)(2,1)}, u32[]{:S(2)}, u32[]{:S(2)}) async-start(bf16[4,32,32,128]{3,2,0,1:T(8,128)(2,1)} %multiply_convert_fusion.5), calls=%async_computation.6 | async-start | bytes 2097152 | tf_op jit(solution)/shard_map/all_to_all | solution.py:279
  597.6 179.0 %reduce-scatter.23.cloned.1.call-start = ((), (), s32[]{:S(2)}) async-start(), calls=%async_computation.27 | async-start | bytes 270336 | tf_op jit(solution)/shard_map/reduce_scatter | solution.py:448
  645.9 130.7 %copy-start.139 = (f32[256,8]{0,1:T(8,128)S(1)}, f32[256,8]{0,1:T(8,128)}, u32[]{:S(2)}) copy-start(f32[256,8]{0,1:T(8,128)} %param.36) | copy-start | bytes 24580
  645.9 130.7 %copy-start.140 = (f32[256,8]{0,1:T(8,128)S(1)}, f32[256,8]{0,1:T(8,128)}, u32[]{:S(2)}) copy-start(f32[256,8]{0,1:T(8,128)} %param.46) | copy-start | bytes 24580
  645.9 130.7 %copy-start.141 = (f32[256,8]{0,1:T(8,128)S(1)}, f32[256,8]{0,1:T(8,128)}, u32[]{:S(2)}) copy-start(f32[256,8]{0,1:T(8,128)} %param.47) | copy-start | bytes 24580
  647.2 275.1 %reduce-scatter.33.cloned.1.call-start = ((), (), s32[]{:S(2)}) async-start(), calls=%async_computation.32 | async-start | bytes 6291456
  776.6 67.4 %copy-start.16 = (f32[16,128,256]{2,1,0:T(8,128)S(1)}, f32[16,128,256]{2,1,0:T(8,128)}, u32[]{:S(2)}) copy-start(f32[16,128,256]{2,1,0:T(8,128)} %copy-done.15) | copy-start | bytes 6291460
  869.8 146.9 %reduce-scatter.19.cloned.1.call-start = ((), (), s32[]{:S(2)}) async-start(), calls=%async_computation.23 | async-start | bytes 6291456 | tf_op jit(solution)/shard_map/reduce_scatter | solution.py:355
  952.7 30.5 %all-to-all-start.5 = ((bf16[2,2,131072]{2,1,0:T(2,128)(2,1)}), bf16[2,2,131072]{2,1,0:T(2,128)(2,1)}, u32[]{:S(2)}, u32[]{:S(2)}) async-start(bf16[2,2,131072]{2,1,0:T(2,128)(2,1)} %reshape.669), calls=%async_computation.5 | async-start | bytes 2097152 | tf_op jit(solution)/shard_map/all_to_all | solution.py:376
  957.3 209.7 %all-gather.11.cloned.1.call-start = ((), (), s32[]{:S(2)}) async-start(), calls=%async_computation.21 | async-start | bytes 3145728 | tf_op jit(solution)/shard_map/all_gather | solution.py:124
  1033.0 28.0 %all-to-all-start.7 = ((bf16[2,2,131072]{2,1,0:T(2,128)(2,1)}), bf16[2,2,131072]{2,1,0:T(2,128)(2,1)S(1)}, u32[]{:S(2)}, u32[]{:S(2)}) async-start(bf16[2,2,131072]{2,1,0:T(2,128)(2,1)} %reshape.671), calls=%async_computation.8 | async-start | bytes 2097152 | tf_op jit(solution)/shard_map/all_to_all | solution.py:377
  1060.9 47.6 %all-to-all-start.3 = ((bf16[2,2,131072]{2,1,0:T(2,128)(2,1)}), bf16[2,2,131072]{2,1,0:T(2,128)(2,1)}, u32[]{:S(2)}, u32[]{:S(2)}) async-start(bf16[2,2,131072]{2,1,0:T(2,128)(2,1)} %reshape.667), calls=%async_computation.3 | async-start | bytes 2097152 | tf_op jit(solution)/shard_map/all_to_all | solution.py:317
  1065.4 111.8 %all-gather.15.cloned.1.call-start = ((), (), s32[]{:S(2)}) async-start(), calls=%async_computation.24 | async-start | bytes 3145728 | tf_op jit(solution)/shard_map/all_gather | solution.py:125
  1108.6 21.7 %all-to-all-start.1 = ((bf16[2,2,131072]{2,1,0:T(2,128)(2,1)}), bf16[2,2,131072]{2,1,0:T(2,128)(2,1)S(1)}, u32[]{:S(2)}, u32[]{:S(2)}) async-start(bf16[2,2,131072]{2,1,0:T(2,128)(2,1)} %reshape.665), calls=%async_computation.1 | async-start | bytes 2097152 | tf_op jit(solution)/shard_map/all_to_all | solution.py:316
  1112.3 147.8 %reduce-scatter.21.cloned.1.call-start = ((), (), s32[]{:S(2)}) async-start(), calls=%async_computation.26 | async-start | bytes 811008 | tf_op jit(solution)/shard_map/reduce_scatter | solution.py:447
  1204.7 18.9 %all-to-all-start.10 = ((bf16[16,64,128]{2,1,0:T(8,128)(2,1)}), bf16[16,64,128]{2,1,0:T(8,128)(2,1)S(1)}, u32[]{:S(2)}, u32[]{:S(2)}) async-start(bf16[16,64,128]{2,1,0:T(8,128)(2,1)} %bitcast.189), calls=%async_computation.11 | async-start | bytes 524288 | tf_op jit(solution)/shard_map/all_to_all | solution.py:34
  1210.4 84.1 %all-gather.13.cloned.1.call-start = ((), (), s32[]{:S(2)}) async-start(), calls=%async_computation.22 | async-start | bytes 3145728 | tf_op jit(solution)/shard_map/all_gather | solution.py:124
  1222.2 37.9 %copy-start.83 = (f32[256,24]{0,1:T(8,128)S(1)}, f32[256,24]{0,1:T(8,128)}, u32[]{:S(2)}) copy-start(f32[256,24]{0,1:T(8,128)} %param.35) | copy-start | bytes 73732
  1222.2 37.9 %copy-start.123 = (f32[256,24]{0,1:T(8,128)S(1)}, f32[256,24]{0,1:T(8,128)}, u32[]{:S(2)}) copy-start(f32[256,24]{0,1:T(8,128)} %param.44) | copy-start | bytes 73732
  1222.2 37.9 %copy-start.124 = (f32[256,24]{0,1:T(8,128)S(1)}, f32[256,24]{0,1:T(8,128)}, u32[]{:S(2)}) copy-start(f32[256,24]{0,1:T(8,128)} %param.45) | copy-start | bytes 73732
  1222.4 39.1 %copy-start.161 = (f32[128]{0:T(128)S(1)}, f32[128]{0:T(128)}, u32[]{:S(2)}) copy-start(f32[128]{0:T(128)} %get-tuple-element.156) | copy-start | bytes 1540
  1222.4 39.1 %copy-start.162 = (f32[128]{0:T(128)S(1)}, f32[128]{0:T(128)}, u32[]{:S(2)}) copy-start(f32[128]{0:T(128)} %get-tuple-element.154) | copy-start | bytes 1540
  1222.5 39.6 %copy-start.165 = (f32[128]{0:T(128)S(1)}, f32[128]{0:T(128)}, u32[]{:S(2)}) copy-start(f32[128]{0:T(128)} %get-tuple-element.132) | copy-start | bytes 1540
  1222.5 39.6 %copy-start.166 = (f32[128]{0:T(128)S(1)}, f32[128]{0:T(128)}, u32[]{:S(2)}) copy-start(f32[128]{0:T(128)} %get-tuple-element.149) | copy-start | bytes 1540
  1222.5 40.2 %copy-start.73 = (f32[64,128]{1,0:T(8,128)S(1)}, f32[64,128]{1,0:T(8,128)}, u32[]{:S(2)}) copy-start(f32[64,128]{1,0:T(8,128)} %param.34) | copy-start | bytes 98308
  1222.5 40.2 %copy-start.115 = (f32[64,128]{1,0:T(8,128)S(1)}, f32[64,128]{1,0:T(8,128)}, u32[]{:S(2)}) copy-start(f32[64,128]{1,0:T(8,128)} %param.42) | copy-start | bytes 98308
  1222.5 40.2 %copy-start.116 = (f32[64,128]{1,0:T(8,128)S(1)}, f32[64,128]{1,0:T(8,128)}, u32[]{:S(2)}) copy-start(f32[64,128]{1,0:T(8,128)} %param.43) | copy-start | bytes 98308
  1223.6 39.9 %copy-start.65 = (f32[128,144]{0,1:T(8,128)S(1)}, f32[128,144]{0,1:T(8,128)}, u32[]{:S(2)}) copy-start(f32[128,144]{0,1:T(8,128)} %param.33) | copy-start | bytes 221188
  1223.6 39.9 %copy-start.90 = (f32[128,144]{0,1:T(8,128)S(1)}, f32[128,144]{0,1:T(8,128)}, u32[]{:S(2)}) copy-start(f32[128,144]{0,1:T(8,128)} %param.40) | copy-start | bytes 221188
  1223.6 39.9 %copy-start.91 = (f32[128,144]{0,1:T(8,128)S(1)}, f32[128,144]{0,1:T(8,128)}, u32[]{:S(2)}) copy-start(f32[128,144]{0,1:T(8,128)} %param.41) | copy-start | bytes 221188
  1223.6 70.9 %copy-start.79 = (f32[16,128]{1,0:T(8,128)S(1)}, f32[16,128]{1,0:T(8,128)}, u32[]{:S(2)}) copy-start(f32[16,128]{1,0:T(8,128)} %copy-done.78) | copy-start | bytes 24580
  1223.6 70.9 %copy-start.95 = (f32[16,128]{1,0:T(8,128)S(1)}, f32[16,128]{1,0:T(8,128)}, u32[]{:S(2)}) copy-start(f32[16,128]{1,0:T(8,128)} %copy-done.94) | copy-start | bytes 24580
  1223.6 70.9 %copy-start.121 = (f32[128]{0:T(128)S(1)}, f32[128]{0:T(128)}, u32[]{:S(2)}) copy-start(f32[128]{0:T(128)} %copy-done.119) | copy-start | bytes 1540
  1223.6 70.9 %copy-start.136 = (f32[128]{0:T(128)S(1)}, f32[128]{0:T(128)}, u32[]{:S(2)}) copy-start(f32[128]{0:T(128)} %copy-done.134) | copy-start | bytes 1540
  1223.6 39.8 %all-to-all-start.9 = ((bf16[16,128,144]{1,2,0:T(8,128)(2,1)}), bf16[16,128,144]{1,2,0:T(8,128)(2,1)S(1)}, u32[]{:S(2)}, u32[]{:S(2)}) async-start(bf16[16,128,144]{1,2,0:T(8,128)(2,1)} %bitcast.188), calls=%async_computation.10 | async-start | bytes 1179648 | tf_op jit(solution)/shard_map/all_to_all | solution.py:34
  1229.8 99.3 %all-gather.17.cloned.1.call-start = ((), (), s32[]{:S(2)}) async-start(), calls=%async_computation.25 | async-start | bytes 3145728 | tf_op jit(solution)/shard_map/all_gather | solution.py:125
  1264.2 41.8 %copy-start.6 = (bf16[16,16,16,128]{3,0,2,1:T(8,128)(2,1)S(1)}, bf16[16,16,16,128]{3,0,2,1:T(8,128)(2,1)}, u32[]{:S(2)}) copy-start(bf16[16,16,16,128]{3,0,2,1:T(8,128)(2,1)} %copy-done.5) | copy-start | bytes 3145732
  1338.6 82.1 %all-to-all-start.8 = ((bf16[16,128,144]{1,2,0:T(8,128)(2,1)}), bf16[16,128,144]{1,2,0:T(8,128)(2,1)}, u32[]{:S(2)}, u32[]{:S(2)}) async-start(bf16[16,128,144]{1,2,0:T(8,128)(2,1)} %bitcast.132), calls=%async_computation.9 | async-start | bytes 1179648 | tf_op jit(solution)/shard_map/all_to_all | solution.py:34
  1377.9 42.1 %copy-start.131 = (f32[12,8]{0,1:T(8,128)S(1)}, f32[12,8]{0,1:T(8,128)}, u32[]{:S(2)}) copy-start(f32[12,8]{0,1:T(8,128)} %param.37) | copy-start | bytes 1156
  1377.9 42.1 %copy-start.147 = (f32[12,8]{0,1:T(8,128)S(1)}, f32[12,8]{0,1:T(8,128)}, u32[]{:S(2)}) copy-start(f32[12,8]{0,1:T(8,128)} %param.48) | copy-start | bytes 1156
  1377.9 42.1 %copy-start.148 = (f32[12,8]{0,1:T(8,128)S(1)}, f32[12,8]{0,1:T(8,128)}, u32[]{:S(2)}) copy-start(f32[12,8]{0,1:T(8,128)} %param.49) | copy-start | bytes 1156
  1377.9 43.9 %copy-start.67 = (f32[128,144]{0,1:T(8,128)S(1)}, f32[128,144]{0,1:T(8,128)}, u32[]{:S(2)}) copy-start(f32[128,144]{0,1:T(8,128)} %param.32) | copy-start | bytes 221188
  1377.9 43.9 %copy-start.92 = (f32[128,144]{0,1:T(8,128)S(1)}, f32[128,144]{0,1:T(8,128)}, u32[]{:S(2)}) copy-start(f32[128,144]{0,1:T(8,128)} %param.38) | copy-start | bytes 221188
  1377.9 43.9 %copy-start.93 = (f32[128,144]{0,1:T(8,128)S(1)}, f32[128,144]{0,1:T(8,128)}, u32[]{:S(2)}) copy-start(f32[128,144]{0,1:T(8,128)} %param.39) | copy-start | bytes 221188
  (135 other events, 682.8 us)
Sparse Core Ops, SparseCore 0:
  137.2 29.4 reduce-scatter.28
  199.3 29.4 reduce-scatter.24
  300.1 29.4 reduce-scatter.30
  380.9 34.7 reduce-scatter.26
  490.7 63.8 all-gather.8
  559.2 75.9 all-gather.6
  647.3 129.2 reduce-scatter.22
  869.9 52.2 reduce-scatter.32
  924.6 65.5 reduce-scatter.18
  1016.8 43.7 all-gather.10
  1083.2 37.1 all-gather.14
  1159.4 100.6 reduce-scatter.20
  1262.3 32.1 all-gather.12
  1295.9 33.0 all-gather.16
where the time goes:
time: 1440 us; the launch traced here: 1430 us
  local copies, waits for them, and re-layouts  473 us (33%)
  blocking collectives  344 us (24%)
  waiting for transfers between devices  296 us (21%)
  matrix products  138 us (10%)
  other arithmetic  112 us (8%)
  starting transfers between devices  48.7 us (3%)
  between operations  17.1 us (1%)
    unnamed x385, local copies, waits for them, and re-layouts  338 us
    reduce_scatter x1, waiting for transfers between devices, per_device(): lax.psum_scatter(proj_grad, ('wide', 'narrow'), scatter_dimension=1, tile...  129 us
    all_gather x1, blocking collectives, per_device(): lax.all_gather(attn_qkv.astype(jnp.bfloat16), ('wide', 'narrow'), axis=1,...  81 us
    all_gather x1, blocking collectives, per_device(): lax.all_gather(vectors.astype(jnp.bfloat16), ('wide', 'narrow'), axis=1,...  70 us
    all_gather x1, blocking collectives, per_device(): lax.all_gather(attn_proj.astype(jnp.bfloat16), ('wide', 'narrow'), axis=1...  64.3 us
    conv_general_dilated x8, matrix products, conv_apply(): lax.conv_general_dilated(inputs, kernel, (1, 1), 'SAME', dimension_number...  55.7 us
    unnamed x1, blocking collectives  40.7 us
    all_gather x2, waiting for transfers between devices, conv_grads(): lax.all_gather(small_grad, 'narrow', axis=3, tiled=True)  30.3 us
  transfers between devices with their start and end apart: 24, of which 9 were waited for; matrix products, arithmetic and copies ran while one was open for 43% of the time, Pallas kernels for 0%

commit v1 on v0

v1 whole, which is shorter than its diff:
```python
import functools
import math

import jax
import jax.numpy as jnp
from jax import lax
from jax.experimental import pallas as pl
from jax.experimental.pallas import tpu as pltpu
from jax.sharding import PartitionSpec as P

GROUPS = 32
STEP_NUMBER = 10
NORM_EPS = 1e-05
ADAM_ONE = 0.9
ADAM_TWO = 0.999
ADAM_EPS = 1e-08
DECAY = 0.01
RATE_CONV = 0.08
RATE_TIME = 0.1
RATE_QKV = 0.2
RATE_PROJ = 1.0
RATE_VECTOR = 1.5
LOG_PERIOD = math.log(10000.0)
PRECISE = lax.Precision.HIGHEST
BF = jnp.bfloat16
F32 = jnp.float32
BLOCK_ROWS = 1024
VMEM_LIMIT = 60 * 2**20
NT = (((1,), (1,)), ((), ()))
TN = (((0,), (0,)), ((), ()))


def dot(a, b, dims=(((1,), (0,)), ((), ()))):
    return lax.dot_general(a, b, dims, preferred_element_type=F32)


def swap_narrow(x):
    return lax.ppermute(x, "narrow", [(0, 1), (1, 0)])


def swap_wide(x, bit):
    count = lax.axis_size("wide")
    return lax.ppermute(x, "wide", [(i, i ^ (1 << bit)) for i in range(count)])


def swap(x, step):
    return swap_narrow(x) if step == "n" else swap_wide(x, step)


def gather_order():
    bits = (lax.axis_size("wide") - 1).bit_length()
    return ["n"] + list(range(bits - 2, 0, -1)) + [bits - 1, 0] if bits > 1 else ["n", 0]


def gather_slots(block, order):
    slots = block[None]
    for step in order:
        slots = jnp.concatenate([slots, swap(slots, step)], axis=0)
    return slots


def slot_of(order, delta_wide, delta_narrow):
    slot = 0
    for i, step in enumerate(order):
        bit = delta_narrow if step == "n" else (delta_wide >> step) & 1
        slot = slot + (bit << i)
    return slot


def scatter_slots(slots, order):
    for step in reversed(order):
        half = slots.shape[0] // 2
        arrived = swap(slots[half:].astype(BF), step)
        slots = slots[:half].astype(F32) + arrived.astype(F32)
    return slots[0]


def slot_table(order):
    here_wide = lax.axis_index("wide")
    here_narrow = lax.axis_index("narrow")
    wide = jnp.arange(lax.axis_size("wide"), dtype=jnp.int32)[:, None] ^ here_wide
    narrow = jnp.arange(lax.axis_size("narrow"), dtype=jnp.int32)[None, :] ^ here_narrow
    return slot_of(order, wide, narrow).reshape(-1)


def device_table(order):
    here_wide = lax.axis_index("wide")
    here_narrow = lax.axis_index("narrow")
    slots = jnp.arange(lax.axis_size("wide") * lax.axis_size("narrow"), dtype=jnp.int32)
    wide = jnp.zeros_like(slots)
    narrow = jnp.zeros_like(slots)
    for i, step in enumerate(order):
        bit = (slots >> i) & 1
        if step == "n":
            narrow = narrow + bit
        else:
            wide = wide + (bit << step)
    return (wide ^ here_wide) * 2 + (narrow ^ here_narrow)


def unpack_kernel(table, src, *outs, parts):
    def body(place, carry):
        slot = table[place]
        for out, (start, stop, joined) in zip(outs, parts):
            block = src[slot, start:stop, :]
            if joined:
                lanes = pl.ds(pl.multiple_of((place & 1) * 128, 128), 128)
                out[place >> 1, :, lanes] = block
            else:
                out[place] = block
        return carry

    lax.fori_loop(0, src.shape[0], body, 0)


def run_unpack(slots, table, parts):
    count, _, width = slots.shape
    shapes = []
    for start, stop, joined in parts:
        shape = (count // 2, stop - start, 256) if joined else (count, stop - start, width)
        shapes.append(jax.ShapeDtypeStruct(shape, slots.dtype))
    return pl.pallas_call(
        functools.partial(unpack_kernel, parts=parts),
        in_specs=[
            pl.BlockSpec(memory_space=pltpu.SMEM),
            pl.BlockSpec(memory_space=pltpu.VMEM),
        ],
        out_specs=[pl.BlockSpec(memory_space=pltpu.VMEM)] * len(parts),
        out_shape=shapes,
        compiler_params=pltpu.CompilerParams(vmem_limit_bytes=VMEM_LIMIT),
    )(table, slots)


def pack_kernel(table, *refs, joined):
    ins = refs[: len(joined)]
    outs = refs[len(joined) :]

    def body(slot, carry):
        place = table[slot]
        for src, out, lanes_joined in zip(ins, outs, joined):
            if lanes_joined:
                lanes = pl.ds(pl.multiple_of((place & 1) * 128, 128), 128)
                out[slot] = src[place >> 1, :, lanes].astype(BF)
            else:
                out[slot] = src[place].astype(BF)
        return carry

    lax.fori_loop(0, outs[0].shape[0], body, 0)


def run_pack(arrays, table, joined):
    shapes = []
    for array, halves in zip(arrays, joined):
        count, rows, width = array.shape
        shape = (count * 2, rows, 128) if halves else (count, rows, width)
        shapes.append(jax.ShapeDtypeStruct(shape, BF))
    return pl.pallas_call(
        functools.partial(pack_kernel, joined=joined),
        in_specs=[pl.BlockSpec(memory_space=pltpu.SMEM)]
        + [pl.BlockSpec(memory_space=pltpu.VMEM)] * len(arrays),
        out_specs=[pl.BlockSpec(memory_space=pltpu.VMEM)] * len(arrays),
        out_shape=shapes,
        compiler_params=pltpu.CompilerParams(vmem_limit_bytes=VMEM_LIMIT),
    )(table, *arrays)


def group_total(s):
    lane = lax.broadcasted_iota(jnp.int32, s.shape, 1)
    width = s.shape[1]
    for k in (1, 2, 4):
        s = s + jnp.where((lane & k) == 0, pltpu.roll(s, width - k, 1), pltpu.roll(s, k, 1))
    return s


def rows_sum(z):
    return jnp.sum(z, axis=0, keepdims=True)


def stack_rows(rows):
    return rows[0] if len(rows) == 1 else jnp.concatenate(rows, axis=0)


def norm_stats(get, n, pixels):
    scale = 1.0 / (8 * pixels)
    mean = group_total(stack_rows([rows_sum(get(m)) for m in range(n)])) * scale
    spread = []
    for m in range(n):
        centered = get(m) - mean[m : m + 1, :]
        spread.append(rows_sum(centered * centered))
    inverse = lax.rsqrt(group_total(stack_rows(spread)) * scale + NORM_EPS)
    return mean, inverse


def sigmoid(v):
    return 1.0 / (1.0 + jnp.exp(-v))


def shift_store(dst, m, value, height, breadth, forward):
    pixels = height * breadth
    channels = value.shape[1]
    column = lax.broadcasted_iota(jnp.int32, value.shape, 0) & (breadth - 1)
    before = jnp.where(column == 0, 0.0, pltpu.roll(value, 1, 0)).astype(BF)
    after = jnp.where(column == breadth - 1, 0.0, pltpu.roll(value, pixels - 1, 0)).astype(BF)
    lo, hi = (before, after) if forward else (after, before)
    rows = slice(breadth, breadth + pixels)
    dst[m, rows, 0:channels] = lo
    dst[m, rows, channels : 2 * channels] = value.astype(BF)
    dst[m, rows, 2 * channels :] = hi


def zero_edges(dst, height, breadth):
    n, rows, width = dst.shape
    edge = jnp.zeros((n, breadth, width), BF)
    dst[:, 0:breadth, :] = edge
    dst[:, rows - breadth :, :] = edge


def join_halves(place, own, other, dst):
    rows = dst.shape[0]

    @pl.when(place == 0)
    def _():
        dst[:, 0:128] = own[...].reshape(rows, 128)
        dst[:, 128:256] = other[...].reshape(rows, 128)

    @pl.when(place != 0)
    def _():
        dst[:, 0:128] = other[...].reshape(rows, 128)
        dst[:, 128:256] = own[...].reshape(rows, 128)


def conv_forward(shifted, kt, n, height, breadth):
    pixels = height * breadth
    total = None
    for p in range(3):
        for q in range(3):
            tap = 3 * p + q
            window = shifted[:, p * breadth : p * breadth + pixels, q * 256 : (q + 1) * 256]
            part = dot(window.reshape(n * pixels, 256), kt[tap * 256 : (tap + 1) * 256, :], NT)
            total = part if total is None else total + part
    return total


def grad_window(shifted, p, n, height, breadth):
    pixels = height * breadth
    start = (2 - p) * breadth
    return shifted[:, start : start + pixels, :].reshape(n * pixels, 768)


def conv_back(shifted, kt, n, height, breadth):
    window = jnp.concatenate(
        [grad_window(shifted, p, n, height, breadth) for p in range(3)], axis=1
    )
    return dot(window, kt[...])


def conv_weight(shifted, act, acc, n, height, breadth):
    for p in range(3):
        window = grad_window(shifted, p, n, height, breadth)
        acc[p * 768 : (p + 1) * 768, :] += dot(window, act, TN)


def first_kernel(sc, xa, xb, kt, vec, c1_o, u1_o, zh_o, inv_o, x_s, shifted, *, n, height, breadth):
    pixels = height * breadth
    join_halves(sc[0], xa, xb, x_s)

    @pl.when(pl.program_id(0) == 0)
    def _():
        zero_edges(shifted, height, breadth)

    def get(m):
        return x_s[m * pixels : (m + 1) * pixels, :].astype(F32)

    mean, inverse = norm_stats(get, n, pixels)
    inv_o[0, 0:n, :] = inverse
    for m in range(n):
        rows = slice(m * pixels, (m + 1) * pixels)
        zh = (get(m) - mean[m : m + 1, :]) * inverse[m : m + 1, :]
        zh_o[rows, :] = zh.astype(BF)
        a1 = zh * vec[0:1, :] + vec[1:2, :]
        u1 = a1 * sigmoid(a1)
        u1_o[rows, :] = u1.astype(BF)
        shift_store(shifted, m, u1, height, breadth, True)
    c1_o[...] = conv_forward(shifted, kt, n, height, breadth)


def middle_kernel(
    sc, c1, te, xa, xb, ga, gb, kt, wqkv, wo, vec, aq_i, ao_i, av_i,
    u2_o, zh2_o, inv2_o, gc2_o, mine_o, send_o, aq, ao, av,
    x_s, gy_s, shifted, h_s, zh3_s, hn_s, qkv_s, o_s, go_s, j_s, gk_s, gv_s,
    *, n, height, breadth, own, which, first_call,
):
    pixels = height * breadth
    total = n * pixels
    step = pl.program_id(0)
    join_halves(sc[0], xa, xb, x_s)
    join_halves(sc[0], ga, gb, gy_s)

    @pl.when(step == 0)
    def _():
        zero_edges(shifted, height, breadth)
        aq[...] = jnp.zeros_like(aq) if first_call else aq_i[...]
        ao[...] = jnp.zeros_like(ao) if first_call else ao_i[...]
        av[...] = jnp.zeros_like(av) if first_call else av_i[...]

    live = []
    for m in range(n):
        rows = slice(m * pixels, (m + 1) * pixels)
        slot = sc[0] * own + step * n + m
        live.append((slot < sc[1 + which]).astype(F32))
        gy_s[rows, :] = (gy_s[rows, :].astype(F32) * live[m]).astype(BF)

    def get_c1(m):
        return c1[m * pixels : (m + 1) * pixels, :] + te[0, m : m + 1, :]

    mean, inverse = norm_stats(get_c1, n, pixels)
    inv2_o[0, 0:n, :] = inverse
    for m in range(n):
        rows = slice(m * pixels, (m + 1) * pixels)
        zh = (get_c1(m) - mean[m : m + 1, :]) * inverse[m : m + 1, :]
        zh2_o[rows, :] = zh.astype(BF)
        a2 = zh * vec[2:3, :] + vec[3:4, :]
        u2 = a2 * sigmoid(a2)
        u2_o[rows, :] = u2.astype(BF)
        shift_store(shifted, m, u2, height, breadth, True)
    h_s[...] = (
        conv_forward(shifted, kt, n, height, breadth) + vec[8:9, :] + x_s[...].astype(F32)
    )

    def get_h(m):
        return h_s[m * pixels : (m + 1) * pixels, :]

    mean, inverse3 = norm_stats(get_h, n, pixels)
    for m in range(n):
        rows = slice(m * pixels, (m + 1) * pixels)
        zh = (get_h(m) - mean[m : m + 1, :]) * inverse3[m : m + 1, :]
        zh3_s[rows, :] = zh
        hn_s[rows, :] = (zh * vec[4:5, :] + vec[5:6, :]).astype(BF)
    for part in range(3):
        lanes = slice(part * 256, (part + 1) * 256)
        projected = dot(hn_s[...], wqkv[lanes, :], NT)
        if part == 0:
            projected = projected + vec[9:10, :]
        if part == 2:
            projected = projected + vec[10:11, :]
        qkv_s[:, lanes] = projected.astype(BF)
    go_s[...] = dot(gy_s[...], wo[...]).astype(BF)

    chunk = min(pixels, 256)
    scale = 1.0 / math.sqrt(256)
    for m in range(n):
        rows = slice(m * pixels, (m + 1) * pixels)
        keys = qkv_s[rows, 256:512]
        values = qkv_s[rows, 512:768]
        for c in range(pixels // chunk):
            part = slice(m * pixels + c * chunk, m * pixels + (c + 1) * chunk)
            queries = qkv_s[part, 0:256]
            scores = dot(queries, keys, NT)
            top = jnp.max(scores, axis=1, keepdims=True)
            exponent = jnp.exp((scores - top) * scale)
            probs = exponent * (1.0 / jnp.sum(exponent, axis=1, keepdims=True))
            low = probs.astype(BF)
            o_s[part, :] = dot(low, values).astype(BF)
            grad_o = go_s[part, :]
            grad_p = dot(grad_o, values, NT)
            inner = jnp.sum(probs * grad_p, axis=1, keepdims=True)
            grad_s = (probs * (grad_p - inner)).astype(BF)
            j_s[part, 0:256] = (dot(grad_s, keys) * scale).astype(BF)
            grad_k = dot(grad_s, queries, TN)
            grad_v = dot(low, grad_o, TN)
            if c == 0:
                gk_s[...] = grad_k
                gv_s[...] = grad_v
            else:
                gk_s[...] += grad_k
                gv_s[...] += grad_v
        j_s[rows, 256:512] = (gk_s[...] * scale).astype(BF)
        j_s[rows, 512:768] = gv_s[...].astype(BF)

    branch = (dot(o_s[...], wo[...], NT) + vec[11:12, :]).astype(BF).astype(F32)
    for m in range(n):
        rows = slice(m * pixels, (m + 1) * pixels)
        out = ((h_s[rows, :] + branch[rows, :]) * live[m]).astype(BF)

        @pl.when(sc[0] == 0)
        def _(out=out, m=m):
            mine_o[m] = out[:, 0:128].reshape(height, breadth, 128)
            send_o[m] = out[:, 128:256].reshape(height, breadth, 128)

        @pl.when(sc[0] != 0)
        def _(out=out, m=m):
            mine_o[m] = out[:, 128:256].reshape(height, breadth, 128)
            send_o[m] = out[:, 0:128].reshape(height, breadth, 128)

    ao[...] += dot(gy_s[...], o_s[...], TN)
    aq[...] += dot(j_s[...], hn_s[...], TN)
    av[9:10, :] += rows_sum(j_s[:, 0:256].astype(F32))
    av[10:11, :] += rows_sum(j_s[:, 512:768].astype(F32))
    av[11:12, :] += rows_sum(gy_s[...].astype(F32))
    grad_hn = dot(j_s[...], wqkv[...]).astype(BF)

    gain = vec[4:5, :]
    one = []
    two = []
    for m in range(n):
        rows = slice(m * pixels, (m + 1) * pixels)
        d = grad_hn[rows, :].astype(F32)
        one.append(rows_sum(d))
        two.append(rows_sum(d * zh3_s[rows, :]))
    one = stack_rows(one)
    two = stack_rows(two)
    av[4:5, :] += rows_sum(two)
    av[5:6, :] += rows_sum(one)
    mean_one = group_total(one * gain) * (1.0 / (8 * pixels))
    mean_two = group_total(two * gain) * (1.0 / (8 * pixels))
    bias = jnp.zeros((1, 256), F32)
    for m in range(n):
        rows = slice(m * pixels, (m + 1) * pixels)
        d = grad_hn[rows, :].astype(F32)
        gz = inverse3[m : m + 1, :] * (
            d * gain - mean_one[m : m + 1, :] - zh3_s[rows, :] * mean_two[m : m + 1, :]
        )
        low = (gz + gy_s[rows, :].astype(F32)).astype(BF)
        gc2_o[rows, :] = low
        bias = bias + rows_sum(low.astype(F32))
    av[8:9, :] += bias


def norm_silu_back(grad_act, zh_ref, inv_ref, gain, shift, n, pixels):
    one = []
    two = []
    grads = []
    for m in range(n):
        rows = slice(m * pixels, (m + 1) * pixels)
        zh = zh_ref[rows, :].astype(F32)
        a = zh * gain + shift
        s = sigmoid(a)
        d = grad_act[rows, :] * (s * (1.0 + a * (1.0 - s)))
        grads.append(d)
        one.append(rows_sum(d))
        two.append(rows_sum(d * zh))
    one = stack_rows(one)
    two = stack_rows(two)
    mean_one = group_total(one * gain) * (1.0 / (8 * pixels))
    mean_two = group_total(two * gain) * (1.0 / (8 * pixels))
    result = []
    for m in range(n):
        rows = slice(m * pixels, (m + 1) * pixels)
        zh = zh_ref[rows, :].astype(F32)
        result.append(
            inv_ref[0, m : m + 1, :]
            * (grads[m] * gain - mean_one[m : m + 1, :] - zh * mean_two[m : m + 1, :])
        )
    return result, rows_sum(one), rows_sum(two)


def second_back_kernel(
    sc, gc2, u2, zh2, inv2, kt, vec, ak_i, av_i,
    gc1_o, ge_o, ak, av, shifted, *, n, height, breadth, first_call,
):
    pixels = height * breadth

    @pl.when(pl.program_id(0) == 0)
    def _():
        zero_edges(shifted, height, breadth)
        ak[...] = jnp.zeros_like(ak) if first_call else ak_i[...]
        av[...] = jnp.zeros_like(av) if first_call else av_i[...]

    for m in range(n):
        rows = slice(m * pixels, (m + 1) * pixels)
        shift_store(shifted, m, gc2[rows, :].astype(F32), height, breadth, False)
    grad_act = conv_back(shifted, kt, n, height, breadth)
    conv_weight(shifted, u2[...], ak, n, height, breadth)
    grads, one, two = norm_silu_back(grad_act, zh2, inv2, vec[2:3, :], vec[3:4, :], n, pixels)
    av[2:3, :] += two
    av[3:4, :] += one
    for m in range(n):
        rows = slice(m * pixels, (m + 1) * pixels)
        low = grads[m].astype(BF)
        gc1_o[rows, :] = low
        ge = rows_sum(low.astype(F32))
        ge_o[0, m : m + 1, :] = ge
        av[6:7, :] += ge
        av[7:8, :] += ge


def first_weight_kernel(sc, gc1, u1, ak_i, ak, shifted, *, n, height, breadth, first_call):
    pixels = height * breadth

    @pl.when(pl.program_id(0) == 0)
    def _():
        zero_edges(shifted, height, breadth)
        ak[...] = jnp.zeros_like(ak) if first_call else ak_i[...]

    for m in range(n):
        rows = slice(m * pixels, (m + 1) * pixels)
        shift_store(shifted, m, gc1[rows, :].astype(F32), height, breadth, False)
    conv_weight(shifted, u1[...], ak, n, height, breadth)


def first_back_kernel(
    sc, gc1, zh1, inv1, gc2, kt, vec, av_i, mine_o, send_o, av, shifted,
    *, n, height, breadth, first_call,
):
    pixels = height * breadth

    @pl.when(pl.program_id(0) == 0)
    def _():
        zero_edges(shifted, height, breadth)
        av[...] = jnp.zeros_like(av) if first_call else av_i[...]

    for m in range(n):
        rows = slice(m * pixels, (m + 1) * pixels)
        shift_store(shifted, m, gc1[rows, :].astype(F32), height, breadth, False)
    grad_act = conv_back(shifted, kt, n, height, breadth)
    grads, one, two = norm_silu_back(grad_act, zh1, inv1, vec[0:1, :], vec[1:2, :], n, pixels)
    av[0:1, :] += two
    av[1:2, :] += one
    for m in range(n):
        rows = slice(m * pixels, (m + 1) * pixels)
        grad = grads[m] + gc2[rows, :].astype(F32)

        @pl.when(sc[0] == 0)
        def _(grad=grad, m=m):
            mine_o[m] = grad[:, 0:128].reshape(height, breadth, 128)
            send_o[m] = grad[:, 128:256].astype(BF).reshape(height, breadth, 128)

        @pl.when(sc[0] != 0)
        def _(grad=grad, m=m):
            mine_o[m] = grad[:, 128:256].reshape(height, breadth, 128)
            send_o[m] = grad[:, 0:128].astype(BF).reshape(height, breadth, 128)


class Group:
    def __init__(self, shape, which):
        self.maps, self.height, self.breadth, self.half = shape
        self.which = which
        self.own = self.maps // 2
        self.pixels = self.height * self.breadth
        self.n = max(1, min(self.own, BLOCK_ROWS // self.pixels))
        self.steps = self.own // self.n
        self.rows = self.n * self.pixels
        self.all_rows = self.own * self.pixels
        self.params = dict(n=self.n, height=self.height, breadth=self.breadth)

    def row_spec(self):
        return pl.BlockSpec((self.rows, 256), lambda i, sc: (i, 0))

    def row_shape(self, dtype):
        return jax.ShapeDtypeStruct((self.all_rows, 256), dtype)

    def map_spec(self, placed):
        steps = self.steps
        shape = (self.n, self.height, self.breadth, 128)
        if placed:
            return pl.BlockSpec(shape, lambda i, sc: (sc[0] * steps + i, 0, 0, 0))
        return pl.BlockSpec(shape, lambda i, sc: (i, 0, 0, 0))

    def map_shape(self, placed, dtype):
        count = self.maps if placed else self.own
        return jax.ShapeDtypeStruct((count, self.height, self.breadth, 128), dtype)

    def stat_spec(self):
        return pl.BlockSpec((1, 8, 256), lambda i, sc: (i, 0, 0))

    def stat_shape(self):
        return jax.ShapeDtypeStruct((self.steps, 8, 256), F32)

    def shifted(self):
        return pltpu.VMEM((self.n, (self.height + 2) * self.breadth, 768), BF)

    def call(self, body, in_specs, out_specs, out_shape, scratch, flops):
        return pl.pallas_call(
            body,
            grid_spec=pltpu.PrefetchScalarGridSpec(
                num_scalar_prefetch=1,
                grid=(self.steps,),
                in_specs=in_specs,
                out_specs=out_specs,
                scratch_shapes=scratch,
            ),
            out_shape=out_shape,
            compiler_params=pltpu.CompilerParams(vmem_limit_bytes=VMEM_LIMIT),
            cost_estimate=pl.CostEstimate(
                flops=flops, bytes_accessed=self.all_rows * 256 * 8, transcendentals=0
            ),
        )


def whole(shape):
    zeros = (0,) * len(shape)
    return pl.BlockSpec(shape, lambda i, sc: zeros)


def run_first(g, sc, x, x_other, kt, vec):
    return g.call(
        functools.partial(first_kernel, **g.params),
        [g.map_spec(True), g.map_spec(False), whole((2304, 256)), whole((16, 256))],
        [g.row_spec(), g.row_spec(), g.row_spec(), g.stat_spec()],
        [g.row_shape(F32), g.row_shape(BF), g.row_shape(BF), g.stat_shape()],
        [pltpu.VMEM((g.rows, 256), BF), g.shifted()],
        2 * g.all_rows * 2304 * 256,
    )(sc, x, x_other, kt, vec)


def run_middle(g, sc, c1, te, x, x_other, gy, gy_other, kt, wqkv, wo, vec, acc, first_call):
    row = g.row_spec()
    big = pltpu.VMEM((g.rows, 256), F32)
    low = pltpu.VMEM((g.rows, 256), BF)
    wide = pltpu.VMEM((g.rows, 768), BF)
    acc_specs = [whole((768, 256)), whole((256, 256)), whole((16, 256))]
    return g.call(
        functools.partial(
            middle_kernel, own=g.own, which=g.which, first_call=first_call, **g.params
        ),
        [
            row, pl.BlockSpec((1, g.n, 256), lambda i, sc: (i, 0, 0)),
            g.map_spec(True), g.map_spec(False), g.map_spec(True), g.map_spec(False),
            whole((2304, 256)), whole((768, 256)), whole((256, 256)), whole((16, 256)),
        ] + acc_specs,
        [row, row, g.stat_spec(), row, g.map_spec(True), g.map_spec(False)] + acc_specs,
        [
            g.row_shape(BF), g.row_shape(BF), g.stat_shape(), g.row_shape(BF),
            g.map_shape(True, BF), g.map_shape(False, BF),
            jax.ShapeDtypeStruct((768, 256), F32), jax.ShapeDtypeStruct((256, 256), F32),
            jax.ShapeDtypeStruct((16, 256), F32),
        ],
        [
            low, low, g.shifted(), big, big, low, wide, low, low, wide,
            pltpu.VMEM((g.pixels, 256), F32), pltpu.VMEM((g.pixels, 256), F32),
        ],
        2 * g.all_rows * 256 * (2304 + 256 * 12 + 6 * g.pixels),
    )(sc, c1, te, x, x_other, gy, gy_other, kt, wqkv, wo, vec, *acc)


def run_second_back(g, sc, gc2, u2, zh2, inv2, kt, vec, acc, first_call):
    row = g.row_spec()
    acc_specs = [whole((2304, 256)), whole((16, 256))]
    return g.call(
        functools.partial(second_back_kernel, first_call=first_call, **g.params),
        [row, row, row, g.stat_spec(), whole((2304, 256)), whole((16, 256))] + acc_specs,
        [row, pl.BlockSpec((1, g.n, 256), lambda i, sc: (i, 0, 0))] + acc_specs,
        [
            g.row_shape(BF), jax.ShapeDtypeStruct((g.steps, g.n, 256), F32),
            jax.ShapeDtypeStruct((2304, 256), F32), jax.ShapeDtypeStruct((16, 256), F32),
        ],
        [g.shifted()],
        4 * g.all_rows * 256 * 2304,
    )(sc, gc2, u2, zh2, inv2, kt, vec, *acc)


def run_first_weight(g, sc, gc1, u1, acc, first_call):
    row = g.row_spec()
    return g.call(
        functools.partial(first_weight_kernel, first_call=first_call, **g.params),
        [row, row, whole((2304, 256))],
        whole((2304, 256)),
        jax.ShapeDtypeStruct((2304, 256), F32),
        [g.shifted()],
        2 * g.all_rows * 256 * 2304,
    )(sc, gc1, u1, acc)


def run_first_back(g, sc, gc1, zh1, inv1, gc2, kt, vec, acc, first_call):
    row = g.row_spec()
    return g.call(
        functools.partial(first_back_kernel, first_call=first_call, **g.params),
        [row, row, g.stat_spec(), row, whole((2304, 256)), whole((16, 256)), whole((16, 256))],
        [g.map_spec(True), g.map_spec(False), whole((16, 256))],
        [g.map_shape(True, F32), g.map_shape(False, BF), jax.ShapeDtypeStruct((16, 256), F32)],
        [g.shifted()],
        2 * g.all_rows * 256 * 2304,
    )(sc, gc1, zh1, inv1, gc2, kt, vec, acc)


def features(steps, index, half_width):
    frequency = jnp.exp(
        (index % half_width).astype(F32) * (-LOG_PERIOD / (half_width - 1))
    )
    angles = steps.astype(F32)[:, None] * frequency[None, :]
    return jax.nn.silu(
        jnp.where(index[None, :] < half_width, jnp.sin(angles), jnp.cos(angles))
    ).astype(BF)


def adam_step(weight, grad, mean, square, rate, decay):
    mean_new = ADAM_ONE * mean + (1.0 - ADAM_ONE) * grad
    square_new = ADAM_TWO * square + (1.0 - ADAM_TWO) * grad * grad
    first_fix = mean_new / (1.0 - ADAM_ONE**STEP_NUMBER)
    second_fix = square_new / (1.0 - ADAM_TWO**STEP_NUMBER)
    weight_new = weight - rate * (first_fix / (jnp.sqrt(second_fix) + ADAM_EPS) + decay * weight)
    return (weight_new, mean_new, square_new)


def other_part(x, here):
    own = x.shape[0] // 2
    part = lax.dynamic_slice_in_dim(x, (1 - here) * own, own, 0)
    return swap_narrow(part)


def put_part(full, arrived, here):
    own = arrived.shape[0]
    return lax.dynamic_update_slice_in_dim(
        full, arrived.astype(full.dtype), (1 - here) * own, 0
    )


def per_device(
    small_maps, large_maps, small_steps, large_steps, live_counts,
    small_cotangent, large_cotangent,
    first_conv, second_conv, time_dense, attn_qkv, attn_proj, vectors,
    first_conv_mean, first_conv_square, second_conv_mean, second_conv_square,
    time_dense_mean, time_dense_square, attn_qkv_mean, attn_qkv_square,
    attn_proj_mean, attn_proj_square, vectors_mean, vectors_square,
):
    n_wide = lax.axis_size("wide")
    here = lax.axis_index("narrow")
    here_wide = lax.axis_index("wide")
    channels = attn_qkv.shape[0]
    half = first_conv.shape[0]
    cols = first_conv.shape[1]
    time_rows = time_dense.shape[0]
    feature_width = time_rows * n_wide
    qcols = attn_qkv.shape[1]
    pcols = attn_proj.shape[1]
    vcols = vectors.shape[1]
    order = gather_order()
    small = Group(small_maps.shape, 0)
    large = Group(large_maps.shape, 1)
    sc = jnp.concatenate([here[None].astype(jnp.int32), live_counts[0]])

    xs = other_part(small_maps, here)
    vec_rows = jnp.pad(
        vectors.astype(BF).T, ((0, 16 - vcols), (0, 128 - vectors.shape[0]))
    )
    g_one = gather_slots(jnp.concatenate([first_conv.astype(BF).T, vec_rows], axis=0), order)
    g_two = gather_slots(
        jnp.concatenate([second_conv.astype(BF).T, time_dense.astype(BF)], axis=0), order
    )
    g_three = gather_slots(
        jnp.concatenate([attn_qkv.astype(BF).T, attn_proj.astype(BF).T], axis=0), order
    )
    table = slot_table(order)
    kt_one, vec = run_unpack(
        g_one, table, ((0, cols, True), (cols, cols + 16, False))
    )
    kt_one = kt_one.reshape(n_wide * cols, 2 * half)
    vec = vec[:, :vcols, :16].reshape(channels, 16).T.astype(F32)
    kt_two, wt = run_unpack(
        g_two, table, ((0, cols, True), (cols, cols + time_rows, True))
    )
    kt_two = kt_two.reshape(n_wide * cols, 2 * half)
    wt = wt.reshape(feature_width, 2 * half)
    (attn,) = run_unpack(g_three, table, ((0, qcols + pcols, False),))
    wqkv = attn[:, :qcols].reshape(3 * channels, channels)
    wo = attn[:, qcols:].reshape(channels, channels)

    own_small = lax.dynamic_slice_in_dim(small_steps, here * small.own, small.own, 0)
    own_large = lax.dynamic_slice_in_dim(large_steps, here * large.own, large.own, 0)
    own_steps = jnp.concatenate([own_small, own_large])
    te = (
        jnp.dot(
            features(own_steps, jnp.arange(feature_width), feature_width // 2),
            wt,
            preferred_element_type=F32,
        )
        + vec[7]
        + vec[6]
    )
    te_small = te[: small.own].reshape(small.steps, small.n, channels)
    te_large = te[small.own :].reshape(large.steps, large.n, channels)

    gs = other_part(small_cotangent, here)
    xl = other_part(large_maps, here)
    gl = other_part(large_cotangent, here)

    zero_q = jnp.zeros((768, 256), F32)
    zero_o = jnp.zeros((256, 256), F32)
    zero_v = jnp.zeros((16, 256), F32)
    zero_k = jnp.zeros((2304, 256), F32)

    s_c1, s_u1, s_zh1, s_inv1 = run_first(small, sc, small_maps, xs, kt_one, vec)
    (s_u2, s_zh2, s_inv2, s_gc2, s_mine, s_send, aq, ao, av) = run_middle(
        small, sc, s_c1, te_small, small_maps, xs, small_cotangent, gs, kt_two, wqkv, wo, vec,
        (zero_q, zero_o, zero_v), True,
    )
    small_out = put_part(s_mine, swap_narrow(s_send), here)
    l_c1, l_u1, l_zh1, l_inv1 = run_first(large, sc, large_maps, xl, kt_one, vec)
    (l_u2, l_zh2, l_inv2, l_gc2, l_mine, l_send, aq, ao, av) = run_middle(
        large, sc, l_c1, te_large, large_maps, xl, large_cotangent, gl, kt_two, wqkv, wo, vec,
        (aq, ao, av), False,
    )
    large_out = put_part(l_mine, swap_narrow(l_send), here)
    devices = device_table(order)
    grads_three = run_pack(
        (aq.reshape(-1, qcols, 256), ao.reshape(-1, pcols, 256)), devices, (False, False)
    )
    sum_three = scatter_slots(jnp.concatenate(grads_three, axis=1), order)

    s_gc1, s_ge, ak, av = run_second_back(
        small, sc, s_gc2, s_u2, s_zh2, s_inv2, kt_two, vec, (zero_k, av), False
    )
    s_mine, s_send, av = run_first_back(
        small, sc, s_gc1, s_zh1, s_inv1, s_gc2, kt_one, vec, av, False
    )
    small_grad = put_part(s_mine, swap_narrow(s_send), here)
    l_gc1, l_ge, ak, av = run_second_back(
        large, sc, l_gc2, l_u2, l_zh2, l_inv2, kt_two, vec, (ak, av), False
    )

    def conv_slots(grad):
        return run_pack((grad.reshape(n_wide, cols, 2 * half),), devices, (True,))[0]

    sum_two = scatter_slots(conv_slots(ak), order)
    ge = jnp.concatenate([s_ge.reshape(small.own, 256), l_ge.reshape(large.own, 256)], axis=0)
    ge_two = jnp.stack([ge[:, :half], ge[:, half:]])
    mine = lax.dynamic_index_in_dim(ge_two, here, 0, keepdims=False)
    other = swap_narrow(lax.dynamic_index_in_dim(ge_two, 1 - here, 0, keepdims=False))
    wide_order = [step for step in order if step != "n"]
    ge_all = gather_slots(jnp.stack([mine, other]), wide_order).reshape(-1, half)
    steps_two = jnp.stack([own_steps, swap_narrow(own_steps)])
    steps_all = gather_slots(steps_two, wide_order).reshape(-1)

    ak_one = run_first_weight(small, sc, s_gc1, s_u1, zero_k, True)
    ak_one = run_first_weight(large, sc, l_gc1, l_u1, ak_one, False)
    sum_one = scatter_slots(conv_slots(ak_one), order)
    l_mine, l_send, av = run_first_back(
        large, sc, l_gc1, l_zh1, l_inv1, l_gc2, kt_one, vec, av, False
    )
    large_grad = put_part(l_mine, swap_narrow(l_send), here)
    vec_blocks = jnp.pad(
        av[:12].T.astype(BF).reshape(-1, vcols, 12), ((0, 0), (0, 8 - vcols), (0, 116))
    )
    sum_vec = scatter_slots(run_pack((vec_blocks,), devices, (False,))[0], order)[:vcols, :12].T

    rows = here_wide * time_rows + jnp.arange(time_rows)
    time_sum = jnp.dot(
        features(steps_all, rows, feature_width // 2).astype(F32).T,
        ge_all,
        precision=PRECISE,
    )
    one_new = adam_step(
        first_conv, sum_one.T, first_conv_mean, first_conv_square, RATE_CONV, DECAY
    )
    two_new = adam_step(
        second_conv, sum_two.T, second_conv_mean, second_conv_square, RATE_CONV, DECAY
    )
    time_new = adam_step(
        time_dense, time_sum, time_dense_mean, time_dense_square, RATE_TIME, DECAY
    )
    qkv_new = adam_step(
        attn_qkv, sum_three[:qcols].T, attn_qkv_mean, attn_qkv_square, RATE_QKV, DECAY
    )
    proj_new = adam_step(
        attn_proj, sum_three[qcols:].T, attn_proj_mean, attn_proj_square, RATE_PROJ, DECAY
    )
    vec_new = adam_step(vectors, sum_vec, vectors_mean, vectors_square, RATE_VECTOR, 0.0)
    return (
        small_out, large_out, small_grad, large_grad,
        *one_new, *two_new, *time_new, *qkv_new, *proj_new, *vec_new,
    )


def solution(mesh):
    maps = P("wide", None, None, "narrow")
    conv = P("narrow", "wide")
    dense = P("wide", "narrow")
    attn = P(None, ("wide", "narrow"))
    return jax.shard_map(
        per_device,
        mesh=mesh,
        in_specs=(
            maps, maps, P("wide"), P("wide"), P("wide", None), maps, maps,
            conv, conv, dense, attn, attn, attn,
            conv, conv, conv, conv, dense, dense, attn, attn, attn, attn, attn, attn,
        ),
        out_specs=(maps,) * 4 + (conv,) * 6 + (dense,) * 3 + (attn,) * 9,
        check_vma=False,
    )
```

time: 1440 us -> 385 us (0.27)
  local copies, waits for them, and re-layouts: 473 us -> 46 us
  blocking collectives: 344 us -> 0 us
  waiting for transfers between devices: 296 us -> 105 us
  Pallas kernels: 0 us -> 150 us
  matrix products: 138 us -> 3.93 us
  other arithmetic: 112 us -> 17.8 us
  between operations: 17.1 us -> 1.95 us
    unnamed x385 -> x93, local copies, waits for them, and re-layouts: 338 us -> 13.9 us
    all_gather x6 -> x0, blocking collectives: 276 us -> none  [the longest x1 81 us: per_device(): lax.all_gather(attn_qkv.astype(jnp.bfloat16), ('wide', 'narrow'), axis=1,...]
    reduce_scatter x3 -> x0, waiting for transfers between devices: 159 us -> none  [the longest x1 129 us: per_device(): lax.psum_scatter(proj_grad, ('wide', 'narrow'), scatter_dimension=1, tile...]
    pallas_call x0 -> x17, Pallas kernels: none -> 150 us  [the longest x2 59.5 us: run_middle(): g.call(functools.partial(middle_kernel, own=g.own, which=g.which, first_c...]
    ppermute x0 -> x53, waiting for transfers between devices: none -> 105 us  [the longest x36 87.8 us: swap_wide(): return lax.ppermute(x, 'wide', [(i, i ^ 1 << bit) for i in range(count)])]
    dot_general x64 -> x2, matrix products: 82.4 us -> 3.93 us  [the longest x1 2.48 us: per_device(): jnp.dot(features(steps_all, rows, feature_width // 2).astype(F32).T, ge_a...]
    all_to_all x10 -> x0, waiting for transfers between devices: 65 us -> none  [the longest x1 21.4 us: per_device(): lax.all_to_all(sent_grad[0], 'narrow', split_axis=1, concat_axis=3, tiled...]
    reduce_sum x54 -> x0, other arithmetic: 61.3 us -> none  [the longest x2 10.1 us: per_device(): jnp.sum(block_low, axis=(0, 1, 2), dtype=jnp.float32)]
  transfers between devices with their start and end apart: 24 -> 53, of which waited for: 9 -> 27; matrix products, arithmetic and copies ran while one was open for 43% -> 16% of each run, Pallas kernels for 0% -> 40%
where the time goes in v1:
time: 385 us; the launch traced here: 378 us
  Pallas kernels  150 us (39%)
  waiting for transfers between devices  105 us (27%)
  starting transfers between devices  52.7 us (14%)
  local copies, waits for them, and re-layouts  46 us (12%)
  other arithmetic  17.8 us (5%)
  matrix products  3.93 us (1%)
    ppermute x36, waiting for transfers between devices, swap_wide(): return lax.ppermute(x, 'wide', [(i, i ^ 1 << bit) for i in range(count)])  87.8 us
    pallas_call x2, Pallas kernels, run_middle(): g.call(functools.partial(middle_kernel, own=g.own, which=g.which, first_c...  59.5 us
    ppermute x36, starting transfers between devices, swap_wide(): return lax.ppermute(x, 'wide', [(i, i ^ 1 << bit) for i in range(count)])  33.2 us
    pallas_call x2, Pallas kernels, run_second_back(): g.call(functools.partial(second_back_kernel, first_call=first_call, **g.p...  25 us
    ppermute x17, starting transfers between devices, swap_narrow(): return lax.ppermute(x, 'narrow', [(0, 1), (1, 0)])  19.5 us
    ppermute x17, waiting for transfers between devices, swap_narrow(): return lax.ppermute(x, 'narrow', [(0, 1), (1, 0)])  17.2 us
    pallas_call x2, Pallas kernels, run_first_back(): g.call(functools.partial(first_back_kernel, first_call=first_call, **g.pa...  16.5 us
    pallas_call x2, Pallas kernels, run_first(): g.call(functools.partial(first_kernel, **g.params), [g.map_spec(True), g....  15.9 us
  transfers between devices with their start and end apart: 53, of which 27 were waited for; matrix products, arithmetic and copies ran while one was open for 16% of the time, Pallas kernels for 40%

profile of v1, /device:TPU:0, one launch (start us, length us, event | category | flops | bytes accessed | tf_op | source)
XLA Modules:
  0.0 377.6 jit_solution(8701528748211397134)
XLA Ops:
  0.7 2.0 constant_dynamic-slice_fusion.3
  2.7 3.0 collective-permute-start
  8.1 2.1 collective-permute-start.6
  11.3 2.0 collective-permute-start.33
  17.5 2.0 constant_dynamic-slice_fusion.1
  20.9 10.3 %collective-permute-done.33 = s32[10]{0:T(128)S(1)} collective-permute-done((s32[10]{0:T(128)S(1)}, s32[10]{0:T(128)S(1)}, u32[]{:S(2)}, u32[]{:S(2)}) %collective-permute-start.33) | collective-permute-done | bytes 72 | tf_op jit(solution)/shard_map/ppermute | solution.py:38
  31.2 1.9 collective-permute-start.34
  33.0 1.8 collective-permute-done.34
  34.8 1.7 collective-permute-start.35
  36.5 1.9 collective-permute-done.35
  38.4 2.8 collective-permute-start.36
  41.2 1.7 collective-permute-done.36
  44.1 1.7 collective-permute-start.12
  47.8 1.8 collective-permute-start.13
  51.8 2.0 collective-permute-start.14
  56.5 2.8 collective-permute-start.15
  60.0 1.7 collective-permute-start.3
  62.8 2.5 collective-permute-done.3
  67.3 11.8 %collective-permute-done.4 = bf16[8,160,128]{2,1,0:T(8,128)(2,1)S(1)} collective-permute-done((bf16[8,160,128]{2,1,0:T(8,128)(2,1)S(1)}, bf16[8,160,128]{2,1,0:T(8,128)(2,1)S(1)}, u32[]{:S(2)}, u32[]{:S(2)}) %collective-permute-start.4) | collective-permute-done | bytes 327712 | tf_op jit(solution)/shard_map/ppermute | solution.py:43
  81.4 1.5 collective-permute-start.18
  83.8 2.0 shard_map.411
  85.8 1.6 slice_bitcast_fusion.wo
  87.4 1.8 slice.240
  89.2 13.6 %collective-permute-done.9 = bf16[8,208,128]{2,1,0:T(8,128)(2,1)S(1)} collective-permute-done((bf16[8,208,128]{2,1,0:T(8,128)(2,1)}, bf16[8,208,128]{2,1,0:T(8,128)(2,1)S(1)}, u32[]{:S(2)}, u32[]{:S(2)}) %collective-permute-start.9) | collective-permute-done | bytes 426016 | tf_op jit(solution)/shard_map/ppermute | solution.py:43
  102.8 1.5 collective-permute-start.19
  107.4 2.8 shard_map.408
  111.7 7.9 %shard_map.409 = (f32[2048,256]{1,0:T(8,128)}, bf16[2048,256]{1,0:T(8,128)(2,1)}, bf16[2048,256]{1,0:T(8,128)(2,1)}, f32[2,8,256]{2,1,0:T(8,128)}) custom-call(s32[3]{0:T(128)} %pad_add_fusion.3.sc, bf16[16,16,16,128]{3,2,1,0:T(8,128)(2,1)} %xa.5, bf16[8,16,16,128]{3,2,1,0:T(8,128)(2,1)} %collective-permute-done.xb, bf16[2304,256]{1,0:T(8,128)(2,1)} %bitcast.143, ...), custom_call_target="tpu_custom_call" | custom-call | flops 2415919104 | bytes 4194304 | tf_op jit(solution)/shard_map/pallas_call | solution.py:596
  119.7 8.0 %shard_map.413 = (f32[2048,256]{1,0:T(8,128)}, bf16[2048,256]{1,0:T(8,128)(2,1)}, bf16[2048,256]{1,0:T(8,128)(2,1)}, f32[2,8,256]{2,1,0:T(8,128)}) custom-call(s32[3]{0:T(128)} %pad_add_fusion.3.sc, bf16[4,32,32,128]{3,2,1,0:T(8,128)(2,1)} %xa.7, bf16[2,32,32,128]{3,2,1,0:T(8,128)(2,1)} %collective-permute-done.18.xb, bf16[2304,256]{1,0:T(8,128)(2,1)} %bitcast.144, ...), custom_call_target="tpu_custom_call" | custom-call | flops 2415919104 | bytes 4194304 | tf_op jit(solution)/shard_map/pallas_call | solution.py:596
  130.9 3.2 shard_map.410
  138.6 27.2 %shard_map.412 = (bf16[2048,256]{1,0:T(8,128)(2,1)}, bf16[2048,256]{1,0:T(8,128)(2,1)}, f32[2,8,256]{2,1,0:T(8,128)}, bf16[2048,256]{1,0:T(8,128)(2,1)}, bf16[16...) custom-call(s32[3]{0:T(128)} %pad_add_fusion.3.sc, ...), custom_call_target="tpu_custom_call" | custom-call | flops 7247757312 | bytes 4194304 | tf_op jit(solution)/shard_map/pallas_call | solution.py:612
  166.9 32.3 %shard_map.414 = (bf16[2048,256]{1,0:T(8,128)(2,1)}, bf16[2048,256]{1,0:T(8,128)(2,1)}, f32[2,8,256]{2,1,0:T(8,128)}, bf16[2048,256]{1,0:T(8,128)(2,1)}, bf16[4,...) custom-call(s32[3]{0:T(128)} %pad_add_fusion.3.sc, ...), custom_call_target="tpu_custom_call" | custom-call | flops 12079595520 | bytes 4194304 | tf_op jit(solution)/shard_map/pallas_call | solution.py:612
  199.2 1.6 collective-permute-start.20
  200.8 1.6 broadcast_in_dim.62.ak_i
  202.4 12.6 %shard_map.415 = (bf16[2048,256]{1,0:T(8,128)(2,1)}, f32[2,4,256]{2,1,0:T(4,128)}, f32[2304,256]{1,0:T(8,128)}, f32[16,256]{1,0:T(8,128)}) custom-call(s32[3]{0:T(128)} %pad_add_fusion.3.sc, bf16[2048,256]{1,0:T(8,128)(2,1)} %get-tuple-element.81.gc2, bf16[2048,256]{1,0:T(8,128)(2,1)} %get-tuple-element.82.u2, bf16[2048,256]{1,0:T(8,128)(2,1)} %get-tuple-element.83.zh2, ...), custom_call_target="tpu_custom_call" | custom-call | flops 4831838208 | bytes 4194304 | tf_op jit(solution)/shard_map/pallas_call | solution.py:639
  215.0 8.3 %shard_map.416 = (f32[16,16,16,128]{3,2,1,0:T(8,128)}, bf16[8,16,16,128]{3,2,1,0:T(8,128)(2,1)}, f32[16,256]{1,0:T(8,128)}) custom-call(s32[3]{0:T(128)} %pad_add_fusion.3.sc, bf16[2048,256]{1,0:T(8,128)(2,1)} %get-tuple-element.86.gc1, bf16[2048,256]{1,0:T(8,128)(2,1)} %get-tuple-element.87.zh1, f32[2,8,256]{2,1,0:T(8,128)} %get-tuple-element.88.inv1, ...), custom_call_target="tpu_custom_call" | custom-call | flops 2415919104 | bytes 4194304 | tf_op jit(solution)/shard_map/pallas_call | solution.py:666
  223.9 7.4 %shard_map.419.ak_i = f32[2304,256]{1,0:T(8,128)} custom-call(s32[3]{0:T(128)} %pad_add_fusion.3.sc, bf16[2048,256]{1,0:T(8,128)(2,1)} %get-tuple-element.86.gc1, bf16[2048,256]{1,0:T(8,128)(2,1)} %get-tuple-element.105.u1, f32[2304,256]{1,0:T(8,128)} %broadcast_in_dim.62.ak_i), custom_call_target="tpu_custom_call" | custom-call | flops 2415919104 | bytes 4194304 | tf_op jit(solution)/shard_map/pallas_call | solution.py:654
  231.3 12.3 %shard_map.417 = (bf16[2048,256]{1,0:T(8,128)(2,1)}, f32[2,1,256]{2,1,0:T(1,128)}, f32[2304,256]{1,0:T(8,128)}, f32[16,256]{1,0:T(8,128)}) custom-call(s32[3]{0:T(128)} %pad_add_fusion.3.sc, bf16[2048,256]{1,0:T(8,128)(2,1)} %get-tuple-element.92.gc2, bf16[2048,256]{1,0:T(8,128)(2,1)} %get-tuple-element.93.u2, bf16[2048,256]{1,0:T(8,128)(2,1)} %get-tuple-element.94.zh2, ...), custom_call_target="tpu_custom_call" | custom-call | flops 4831838208 | bytes 4194304 | tf_op jit(solution)/shard_map/pallas_call | solution.py:639
  243.7 7.6 %shard_map.420 = f32[2304,256]{1,0:T(8,128)} custom-call(s32[3]{0:T(128)} %pad_add_fusion.3.sc, bf16[2048,256]{1,0:T(8,128)(2,1)} %get-tuple-element.98.gc1, bf16[2048,256]{1,0:T(8,128)(2,1)} %get-tuple-element.104.u1, f32[2304,256]{1,0:T(8,128)} %shard_map.419.ak_i), custom_call_target="tpu_custom_call" | custom-call | flops 2415919104 | bytes 4194304 | tf_op jit(solution)/shard_map/pallas_call | solution.py:654
  251.3 3.1 shard_map.421
  255.5 3.2 shard_map.422
  260.5 1.5 collective-permute-start.38
  262.0 2.2 shard_map.423
  266.3 8.2 %shard_map.418 = (f32[4,32,32,128]{3,2,1,0:T(8,128)}, bf16[2,32,32,128]{3,2,1,0:T(8,128)(2,1)}, f32[16,256]{1,0:T(8,128)}) custom-call(s32[3]{0:T(128)} %pad_add_fusion.3.sc, bf16[2048,256]{1,0:T(8,128)(2,1)} %get-tuple-element.98.gc1, bf16[2048,256]{1,0:T(8,128)(2,1)} %get-tuple-element.99.zh1, f32[2,8,256]{2,1,0:T(8,128)} %get-tuple-element.100.inv1, ...), custom_call_target="tpu_custom_call" | custom-call | flops 2415919104 | bytes 4194304 | tf_op jit(solution)/shard_map/pallas_call | solution.py:666
  277.3 1.5 pad.9.refs_0_
  278.8 1.7 shard_map.424
  284.6 2.9 collective-permute-done.39
  287.6 4.5 %collective-permute-done.49 = bf16[8,8,128]{2,1,0:T(8,128)(2,1)S(1)} collective-permute-done((bf16[8,8,128]{2,1,0:T(8,128)(2,1)S(1)}, bf16[8,8,128]{2,1,0:T(8,128)(2,1)S(1)}, u32[]{:S(2)}, u32[]{:S(2)}) %collective-permute-start.49) | collective-permute-done | bytes 16416 | tf_op jit(solution)/shard_map/ppermute | solution.py:43
  293.7 2.2 collective-permute-done.50
  296.7 3.1 collective-permute-done.40
  299.8 3.6 collective-permute-done.51
  304.6 2.4 collective-permute-done.52
  308.2 2.9 collective-permute-start.44
  314.2 2.2 collective-permute-start.45
  317.0 1.6 collective-permute-done.45
  320.0 1.9 collective-permute-start.46
  322.5 1.6 reshape.215
  324.8 2.5 multiply_subtract_fusion.2
  333.2 2.4 collective-permute-start.24
  336.8 19.9 %collective-permute-done.24 = bf16[8,144,128]{2,1,0:T(8,128)(2,1)S(1)} collective-permute-done((bf16[8,144,128]{2,1,0:T(8,128)(2,1)S(1)}, bf16[8,144,128]{2,1,0:T(8,128)(2,1)S(1)}, u32[]{:S(2)}, u32[]{:S(2)}) %collective-permute-start.24) | collective-permute-done | bytes 294944 | tf_op jit(solution)/shard_map/ppermute | solution.py:43
  357.6 4.5 %collective-permute-done.29 = bf16[8,144,128]{2,1,0:T(8,128)(2,1)S(1)} collective-permute-done((bf16[8,144,128]{2,1,0:T(8,128)(2,1)S(1)}, bf16[8,144,128]{2,1,0:T(8,128)(2,1)S(1)}, u32[]{:S(2)}, u32[]{:S(2)}) %collective-permute-start.29) | collective-permute-done | bytes 294944 | tf_op jit(solution)/shard_map/ppermute | solution.py:43
  362.2 1.7 collective-permute-start.30
  364.0 3.9 %collective-permute-done.30 = bf16[4,144,128]{2,1,0:T(8,128)(2,1)S(1)} collective-permute-done((bf16[4,144,128]{2,1,0:T(8,128)(2,1)S(1)}, bf16[4,144,128]{2,1,0:T(8,128)(2,1)S(1)}, u32[]{:S(2)}, u32[]{:S(2)}) %collective-permute-start.30) | collective-permute-done | bytes 147488 | tf_op jit(solution)/shard_map/ppermute | solution.py:43
  369.2 3.1 collective-permute-done.31
  374.0 2.4 collective-permute-done.32
  (281 shorter events, 72.6 us)
Async XLA Ops:
  0.7 13.9 %copy-start.17 = (f32[256,8]{0,1:T(8,128)S(1)}, f32[256,8]{0,1:T(8,128)}, u32[]{:S(2)}) copy-start(f32[256,8]{0,1:T(8,128)} %param.36) | copy-start | bytes 24580
  0.7 13.9 %copy-start.11 = (f32[256,24]{0,1:T(8,128)S(1)}, f32[256,24]{0,1:T(8,128)}, u32[]{:S(2)}) copy-start(f32[256,24]{0,1:T(8,128)} %param.35) | copy-start | bytes 73732
  2.7 109.1 %collective-permute-start = (bf16[8,16,16,128]{3,2,1,0:T(8,128)(2,1)}, bf16[8,16,16,128]{3,2,1,0:T(8,128)(2,1)}, u32[]{:S(2)}, u32[]{:S(2)}) collective-permute-start(bf16[8,16,16,128]{3,2,1,0:T(8,128)(2,1)} %constant_dynamic-slice_fusion.3), channel_id=1, source_target_pairs={{0,1},{1,0},{2,3},{3,2},{4,5},{5,4},{6,7},{7,6},{8,9},{9,8},{10,11... | collective-permute-start | bytes 1572872 | tf_op jit(solution)/shard_map/ppermute | solution.py:38
  7.2 43.0 %collective-permute-start.1 = (bf16[1,160,128]{2,1,0:T(8,128)(2,1)S(1)}, bf16[1,160,128]{2,1,0:T(8,128)(2,1)S(1)}, u32[]{:S(2)}, u32[]{:S(2)}) collective-permute-start(bf16[1,160,128]{2,1,0:T(8,128)(2,1)S(1)} %fusion.27), channel_id=1, source_target_pairs={{0,1},{1,0},{2,3},{3,2},{4,5},{5,4},{6,7},{7,6},{8,9},{9,8},{10,11... | collective-permute-start | bytes 122888 | tf_op jit(solution)/shard_map/ppermute | solution.py:38
  8.1 46.4 %collective-permute-start.6 = (bf16[1,208,128]{2,1,0:T(8,128)(2,1)S(1)}, bf16[1,208,128]{2,1,0:T(8,128)(2,1)S(1)}, u32[]{:S(2)}, u32[]{:S(2)}) collective-permute-start(bf16[1,208,128]{2,1,0:T(8,128)(2,1)S(1)} %maximum_bitcast_fusion), channel_id=1, source_target_pairs={{0,1},{1,0},{2,3},{3,2},{4,5},{5,4},{6,7},{7,6},{8,9},{9,8},{10,11... | collective-permute-start | bytes 159752 | tf_op jit(solution)/shard_map/ppermute | solution.py:38
  11.0 125.3 %collective-permute-start.11 = (bf16[8,16,16,128]{3,2,1,0:T(8,128)(2,1)}, bf16[8,16,16,128]{3,2,1,0:T(8,128)(2,1)}, u32[]{:S(2)}, u32[]{:S(2)}) collective-permute-start(bf16[8,16,16,128]{3,2,1,0:T(8,128)(2,1)} %constant_dynamic-slice_fusion.2), channel_id=1, source_target_pairs={{0,1},{1,0},{2,3},{3,2},{4,5},{5,4},{6,7},{7,6},{8,9},{9,8},{10,11... | collective-permute-start | bytes 1572872 | tf_op jit(solution)/shard_map/ppermute | solution.py:38
  11.3 19.9 %collective-permute-start.33 = (s32[10]{0:T(128)S(1)}, s32[10]{0:T(128)S(1)}, u32[]{:S(2)}, u32[]{:S(2)}) collective-permute-start(s32[10]{0:T(128)S(1)} %get-tuple-element.133), channel_id=1, source_target_pairs={{0,1},{1,0},{2,3},{3,2},{4,5},{5,4},{6,7},{7,6},{8,9},{9,8},{10,11... | collective-permute-start | bytes 128 | tf_op jit(solution)/shard_map/ppermute | solution.py:38
  31.2 3.6 collective-permute-start.34
  34.8 3.6 collective-permute-start.35
  38.4 4.5 %collective-permute-start.36 = (s32[4,2,10]{2,1,0:T(2,128)S(1)}, s32[4,2,10]{2,1,0:T(2,128)S(1)}, u32[]{:S(2)}, u32[]{:S(2)}) collective-permute-start(s32[4,2,10]{2,1,0:T(2,128)S(1)} %pad_add_fusion.1), channel_id=1, source_target_pairs={{0,16},{2,18},{4,20},{6,22},{8,24},{10,26},{12,28},{14,30},{16,0},... | collective-permute-start | bytes 968 | tf_op jit(solution)/shard_map/ppermute | solution.py:43
  42.9 1.2 collective-permute-start.37
  44.1 3.7 collective-permute-start.12
  47.8 4.0 %collective-permute-start.13 = (bf16[2,32,256]{2,1,0:T(8,128)(2,1)S(1)}, bf16[2,32,256]{2,1,0:T(8,128)(2,1)S(1)}, u32[]{:S(2)}, u32[]{:S(2)}) collective-permute-start(bf16[2,32,256]{2,1,0:T(8,128)(2,1)S(1)} %pad_maximum_fusion.10), channel_id=1, source_target_pairs={{0,8},{2,10},{4,12},{6,14},{8,0},{10,2},{12,4},{14,6},{16,24},{18,... | collective-permute-start | bytes 98312 | tf_op jit(solution)/shard_map/ppermute | solution.py:43
  50.2 9.7 %collective-permute-start.2 = (bf16[2,160,128]{2,1,0:T(8,128)(2,1)S(1)}, bf16[2,160,128]{2,1,0:T(8,128)(2,1)S(1)}, u32[]{:S(2)}, u32[]{:S(2)}) collective-permute-start(bf16[2,160,128]{2,1,0:T(8,128)(2,1)S(1)} %pad_maximum_fusion.7), channel_id=1, source_target_pairs={{0,8},{2,10},{4,12},{6,14},{8,0},{10,2},{12,4},{14,6},{16,24},{18,... | collective-permute-start | bytes 245768 | tf_op jit(solution)/shard_map/ppermute | solution.py:43
  51.8 4.6 %collective-permute-start.14 = (bf16[4,32,256]{2,1,0:T(8,128)(2,1)S(1)}, bf16[4,32,256]{2,1,0:T(8,128)(2,1)S(1)}, u32[]{:S(2)}, u32[]{:S(2)}) collective-permute-start(bf16[4,32,256]{2,1,0:T(8,128)(2,1)S(1)} %pad_maximum_fusion.8), channel_id=1, source_target_pairs={{0,4},{2,6},{4,0},{6,2},{8,12},{10,14},{12,8},{14,10},{16,20},{18,... | collective-permute-start | bytes 196616 | tf_op jit(solution)/shard_map/ppermute | solution.py:43
  54.5 7.8 %collective-permute-start.7 = (bf16[2,208,128]{2,1,0:T(8,128)(2,1)S(1)}, bf16[2,208,128]{2,1,0:T(8,128)(2,1)S(1)}, u32[]{:S(2)}, u32[]{:S(2)}) collective-permute-start(bf16[2,208,128]{2,1,0:T(8,128)(2,1)S(1)} %pad_maximum_fusion.6), channel_id=1, source_target_pairs={{0,8},{2,10},{4,12},{6,14},{8,0},{10,2},{12,4},{14,6},{16,24},{18,... | collective-permute-start | bytes 319496 | tf_op jit(solution)/shard_map/ppermute | solution.py:43
  56.5 10.0 %collective-permute-start.15 = (bf16[8,32,256]{2,1,0:T(8,128)(2,1)S(1)}, bf16[8,32,256]{2,1,0:T(8,128)(2,1)S(1)}, u32[]{:S(2)}, u32[]{:S(2)}) collective-permute-start(bf16[8,32,256]{2,1,0:T(8,128)(2,1)S(1)} %pad_maximum_fusion.4), channel_id=1, source_target_pairs={{0,16},{2,18},{4,20},{6,22},{8,24},{10,26},{12,28},{14,30},{16,0},... | collective-permute-start | bytes 393224 | tf_op jit(solution)/shard_map/ppermute | solution.py:43
  60.0 5.4 %collective-permute-start.3 = (bf16[4,160,128]{2,1,0:T(8,128)(2,1)S(1)}, bf16[4,160,128]{2,1,0:T(8,128)(2,1)S(1)}, u32[]{:S(2)}, u32[]{:S(2)}) collective-permute-start(bf16[4,160,128]{2,1,0:T(8,128)(2,1)S(1)} %pad_maximum_fusion.3), channel_id=1, source_target_pairs={{0,4},{2,6},{4,0},{6,2},{8,12},{10,14},{12,8},{14,10},{16,20},{18,... | collective-permute-start | bytes 491528 | tf_op jit(solution)/shard_map/ppermute | solution.py:43
  62.3 17.5 %collective-permute-start.8 = (bf16[4,208,128]{2,1,0:T(8,128)(2,1)S(1)}, bf16[4,208,128]{2,1,0:T(8,128)(2,1)S(1)}, u32[]{:S(2)}, u32[]{:S(2)}) collective-permute-start(bf16[4,208,128]{2,1,0:T(8,128)(2,1)S(1)} %pad_maximum_fusion.2), channel_id=1, source_target_pairs={{0,4},{2,6},{4,0},{6,2},{8,12},{10,14},{12,8},{14,10},{16,20},{18,... | collective-permute-start | bytes 638984 | tf_op jit(solution)/shard_map/ppermute | solution.py:43
  65.4 13.6 %collective-permute-start.4 = (bf16[8,160,128]{2,1,0:T(8,128)(2,1)S(1)}, bf16[8,160,128]{2,1,0:T(8,128)(2,1)S(1)}, u32[]{:S(2)}, u32[]{:S(2)}) collective-permute-start(bf16[8,160,128]{2,1,0:T(8,128)(2,1)S(1)} %pad_maximum_fusion.1), channel_id=1, source_target_pairs={{0,16},{2,18},{4,20},{6,22},{8,24},{10,26},{12,28},{14,30},{16,0},... | collective-permute-start | bytes 983048 | tf_op jit(solution)/shard_map/ppermute | solution.py:43
  66.5 15.0 %collective-permute-start.16 = (bf16[16,32,256]{2,1,0:T(8,128)(2,1)S(1)}, bf16[16,32,256]{2,1,0:T(8,128)(2,1)S(1)}, u32[]{:S(2)}, u32[]{:S(2)}) collective-permute-start(bf16[16,32,256]{2,1,0:T(8,128)(2,1)S(1)} %get-tuple-element.142), channel_id=1, source_target_pairs={{0,2},{2,0},{4,6},{6,4},{8,10},{10,8},{12,14},{14,12},{16,18},{18,... | collective-permute-start | bytes 786440 | tf_op jit(solution)/shard_map/ppermute | solution.py:43
  79.8 25.3 %collective-permute-start.5 = (bf16[16,160,128]{2,1,0:T(8,128)(2,1)}, bf16[16,160,128]{2,1,0:T(8,128)(2,1)}, u32[]{:S(2)}, u32[]{:S(2)}) collective-permute-start(bf16[16,160,128]{2,1,0:T(8,128)(2,1)} %get-tuple-element.136), channel_id=1, source_target_pairs={{0,2},{2,0},{4,6},{6,4},{8,10},{10,8},{12,14},{14,12},{16,18},{18,... | collective-permute-start | bytes 1966088 | tf_op jit(solution)/shard_map/ppermute | solution.py:43
  80.7 22.1 %collective-permute-start.9 = (bf16[8,208,128]{2,1,0:T(8,128)(2,1)}, bf16[8,208,128]{2,1,0:T(8,128)(2,1)S(1)}, u32[]{:S(2)}, u32[]{:S(2)}) collective-permute-start(bf16[8,208,128]{2,1,0:T(8,128)(2,1)} %pad_maximum_fusion), channel_id=1, source_target_pairs={{0,16},{2,18},{4,20},{6,22},{8,24},{10,26},{12,28},{14,30},{16,0},... | collective-permute-start | bytes 1277960 | tf_op jit(solution)/shard_map/ppermute | solution.py:43
  81.4 38.2 %collective-permute-start.18 = (bf16[2,32,32,128]{3,2,1,0:T(8,128)(2,1)}, bf16[2,32,32,128]{3,2,1,0:T(8,128)(2,1)}, u32[]{:S(2)}, u32[]{:S(2)}) collective-permute-start(bf16[2,32,32,128]{3,2,1,0:T(8,128)(2,1)} %constant_dynamic-slice_fusion.1), channel_id=1, source_target_pairs={{0,1},{1,0},{2,3},{3,2},{4,5},{5,4},{6,7},{7,6},{8,9},{9,8},{10,11... | collective-permute-start | bytes 1572872 | tf_op jit(solution)/shard_map/ppermute | solution.py:38
  102.8 64.2 %collective-permute-start.19 = (bf16[2,32,32,128]{3,2,1,0:T(8,128)(2,1)}, bf16[2,32,32,128]{3,2,1,0:T(8,128)(2,1)}, u32[]{:S(2)}, u32[]{:S(2)}) collective-permute-start(bf16[2,32,32,128]{3,2,1,0:T(8,128)(2,1)} %constant_dynamic-slice_fusion), channel_id=1, source_target_pairs={{0,1},{1,0},{2,3},{3,2},{4,5},{5,4},{6,7},{7,6},{8,9},{9,8},{10,11... | collective-permute-start | bytes 1572872 | tf_op jit(solution)/shard_map/ppermute | solution.py:38
  105.2 23.3 %collective-permute-start.10 = (bf16[16,208,128]{2,1,0:T(8,128)(2,1)}, bf16[16,208,128]{2,1,0:T(8,128)(2,1)}, u32[]{:S(2)}, u32[]{:S(2)}) collective-permute-start(bf16[16,208,128]{2,1,0:T(8,128)(2,1)} %get-tuple-element.134), channel_id=1, source_target_pairs={{0,2},{2,0},{4,6},{6,4},{8,10},{10,8},{12,14},{14,12},{16,18},{18,... | collective-permute-start | bytes 2555912 | tf_op jit(solution)/shard_map/ppermute | solution.py:43
  165.8 165.1 %collective-permute-start.17 = (bf16[8,16,16,128]{3,2,1,0:T(8,128)(2,1)}, bf16[8,16,16,128]{3,2,1,0:T(8,128)(2,1)S(1)}, u32[]{:S(2)}, u32[]{:S(2)}) collective-permute-start(bf16[8,16,16,128]{3,2,1,0:T(8,128)(2,1)} %get-tuple-element.74), channel_id=1, source_target_pairs={{0,1},{1,0},{2,3},{3,2},{4,5},{5,4},{6,7},{7,6},{8,9},{9,8},{10,11... | collective-permute-start | bytes 1572872 | tf_op jit(solution)/shard_map/ppermute | solution.py:38
  199.2 137.5 %collective-permute-start.20 = (bf16[2,32,32,128]{3,2,1,0:T(8,128)(2,1)}, bf16[2,32,32,128]{3,2,1,0:T(8,128)(2,1)S(1)}, u32[]{:S(2)}, u32[]{:S(2)}) collective-permute-start(bf16[2,32,32,128]{3,2,1,0:T(8,128)(2,1)} %get-tuple-element.80), channel_id=1, source_target_pairs={{0,1},{1,0},{2,3},{3,2},{4,5},{5,4},{6,7},{7,6},{8,9},{9,8},{10,11... | collective-permute-start | bytes 1572872 | tf_op jit(solution)/shard_map/ppermute | solution.py:38
  223.3 106.0 %collective-permute-start.21 = (bf16[8,16,16,128]{3,2,1,0:T(8,128)(2,1)}, bf16[8,16,16,128]{3,2,1,0:T(8,128)(2,1)S(1)}, u32[]{:S(2)}, u32[]{:S(2)}) collective-permute-start(bf16[8,16,16,128]{3,2,1,0:T(8,128)(2,1)} %get-tuple-element.91), channel_id=1, source_target_pairs={{0,1},{1,0},{2,3},{3,2},{4,5},{5,4},{6,7},{7,6},{8,9},{9,8},{10,11... | collective-permute-start | bytes 1572872 | tf_op jit(solution)/shard_map/ppermute | solution.py:38
  260.5 20.8 %collective-permute-start.38 = (f32[10,128]{1,0:T(8,128)}, f32[10,128]{1,0:T(8,128)}, u32[]{:S(2)}, u32[]{:S(2)}) collective-permute-start(f32[10,128]{1,0:T(8,128)} %get-tuple-element.161), channel_id=1, source_target_pairs={{0,1},{1,0},{2,3},{3,2},{4,5},{5,4},{6,7},{7,6},{8,9},{9,8},{10,11... | collective-permute-start | bytes 15368 | tf_op jit(solution)/shard_map/ppermute | solution.py:38
  266.2 40.9 %collective-permute-start.43 = (bf16[16,32,256]{2,1,0:T(8,128)(2,1)S(1)}, bf16[16,32,256]{2,1,0:T(8,128)(2,1)}, u32[]{:S(2)}, u32[]{:S(2)}) collective-permute-start(bf16[16,32,256]{2,1,0:T(8,128)(2,1)S(1)} %slice.266), channel_id=1, source_target_pairs={{0,2},{2,0},{4,6},{6,4},{8,10},{10,8},{12,14},{14,12},{16,18},{18,... | collective-permute-start | bytes 786440 | tf_op jit(solution)/shard_map/ppermute | solution.py:43
  277.3 33.8 %copy-start.21 = (f32[12,8]{0,1:T(8,128)S(1)}, f32[12,8]{0,1:T(8,128)}, u32[]{:S(2)}) copy-start(f32[12,8]{0,1:T(8,128)} %param.37) | copy-start | bytes 1156
  277.3 33.8 %copy-start.25 = (f32[12,8]{0,1:T(8,128)S(1)}, f32[12,8]{0,1:T(8,128)}, u32[]{:S(2)}) copy-start(f32[12,8]{0,1:T(8,128)} %param.48) | copy-start | bytes 1156
  277.3 33.8 %copy-start.26 = (f32[12,8]{0,1:T(8,128)S(1)}, f32[12,8]{0,1:T(8,128)}, u32[]{:S(2)}) copy-start(f32[12,8]{0,1:T(8,128)} %param.49) | copy-start | bytes 1156
  281.3 2.5 collective-permute-start.48
  283.8 3.7 collective-permute-start.39
  287.5 4.6 %collective-permute-start.49 = (bf16[8,8,128]{2,1,0:T(8,128)(2,1)S(1)}, bf16[8,8,128]{2,1,0:T(8,128)(2,1)S(1)}, u32[]{:S(2)}, u32[]{:S(2)}) collective-permute-start(bf16[8,8,128]{2,1,0:T(8,128)(2,1)S(1)} %slice.374), channel_id=1, source_target_pairs={{0,16},{2,18},{4,20},{6,22},{8,24},{10,26},{12,28},{14,30},{16,0},... | collective-permute-start | bytes 49160 | tf_op jit(solution)/shard_map/ppermute | solution.py:43
  292.2 3.7 collective-permute-start.50
  295.9 3.9 %collective-permute-start.40 = (f32[2,2,10,128]{3,2,1,0:T(8,128)S(1)}, f32[2,2,10,128]{3,2,1,0:T(8,128)S(1)}, u32[]{:S(2)}, u32[]{:S(2)}) collective-permute-start(f32[2,2,10,128]{3,2,1,0:T(8,128)S(1)} %pad_maximum_fusion.11), channel_id=1, source_target_pairs={{0,4},{2,6},{4,0},{6,2},{8,12},{10,14},{12,8},{14,10},{16,20},{18,... | collective-permute-start | bytes 61448 | tf_op jit(solution)/shard_map/ppermute | solution.py:43
  299.8 3.6 collective-permute-start.51
  303.4 3.6 collective-permute-start.52
  307.0 5.3 %collective-permute-start.41 = (f32[4,2,10,128]{3,2,1,0:T(8,128)S(1)}, f32[4,2,10,128]{3,2,1,0:T(8,128)S(1)}, u32[]{:S(2)}, u32[]{:S(2)}) collective-permute-start(f32[4,2,10,128]{3,2,1,0:T(8,128)S(1)} %pad_maximum_fusion.9), channel_id=1, source_target_pairs={{0,16},{2,18},{4,20},{6,22},{8,24},{10,26},{12,28},{14,30},{16,0},... | collective-permute-start | bytes 122888 | tf_op jit(solution)/shard_map/ppermute | solution.py:43
  308.1 16.7 %copy-start.18 = (f32[64,128]{1,0:T(8,128)S(1)}, f32[64,128]{1,0:T(8,128)}, u32[]{:S(2)}) copy-start(f32[64,128]{1,0:T(8,128)} %param.34) | copy-start | bytes 98308
  308.2 5.9 %collective-permute-start.44 = (bf16[8,32,256]{2,1,0:T(8,128)(2,1)S(1)}, bf16[8,32,256]{2,1,0:T(8,128)(2,1)S(1)}, u32[]{:S(2)}, u32[]{:S(2)}) collective-permute-start(bf16[8,32,256]{2,1,0:T(8,128)(2,1)S(1)} %slice.367), channel_id=1, source_target_pairs={{0,16},{2,18},{4,20},{6,22},{8,24},{10,26},{12,28},{14,30},{16,0},... | collective-permute-start | bytes 393224 | tf_op jit(solution)/shard_map/ppermute | solution.py:43
  312.4 18.6 %collective-permute-start.22 = (bf16[2,32,32,128]{3,2,1,0:T(8,128)(2,1)}, bf16[2,32,32,128]{3,2,1,0:T(8,128)(2,1)S(1)}, u32[]{:S(2)}, u32[]{:S(2)}) collective-permute-start(bf16[2,32,32,128]{3,2,1,0:T(8,128)(2,1)} %get-tuple-element.103), channel_id=1, source_target_pairs={{0,1},{1,0},{2,3},{3,2},{4,5},{5,4},{6,7},{7,6},{8,9},{9,8},{10,11... | collective-permute-start | bytes 1572872 | tf_op jit(solution)/shard_map/ppermute | solution.py:38
  314.1 13.9 %copy-start.12 = (f32[256,24]{0,1:T(8,128)S(1)}, f32[256,24]{0,1:T(8,128)}, u32[]{:S(2)}) copy-start(f32[256,24]{0,1:T(8,128)} %param.35) | copy-start | bytes 73732
  314.2 4.5 %collective-permute-start.45 = (bf16[4,32,256]{2,1,0:T(8,128)(2,1)S(1)}, bf16[4,32,256]{2,1,0:T(8,128)(2,1)S(1)}, u32[]{:S(2)}, u32[]{:S(2)}) collective-permute-start(bf16[4,32,256]{2,1,0:T(8,128)(2,1)S(1)} %slice.370), channel_id=1, source_target_pairs={{0,4},{2,6},{4,0},{6,2},{8,12},{10,14},{12,8},{14,10},{16,20},{18,... | collective-permute-start | bytes 196616 | tf_op jit(solution)/shard_map/ppermute | solution.py:43
  318.6 1.3 collective-permute-start.42
  320.0 4.2 %collective-permute-start.46 = (bf16[2,32,256]{2,1,0:T(8,128)(2,1)S(1)}, bf16[2,32,256]{2,1,0:T(8,128)(2,1)S(1)}, u32[]{:S(2)}, u32[]{:S(2)}) collective-permute-start(bf16[2,32,256]{2,1,0:T(8,128)(2,1)S(1)} %slice.373), channel_id=1, source_target_pairs={{0,8},{2,10},{4,12},{6,14},{8,0},{10,2},{12,4},{14,6},{16,24},{18,... | collective-permute-start | bytes 98312 | tf_op jit(solution)/shard_map/ppermute | solution.py:43
  324.2 3.8 %collective-permute-start.47 = (bf16[1,32,256]{2,1,0:T(8,128)(2,1)S(1)}, bf16[1,32,256]{2,1,0:T(8,128)(2,1)S(1)}, u32[]{:S(2)}, u32[]{:S(2)}) collective-permute-start(bf16[1,32,256]{2,1,0:T(8,128)(2,1)S(1)} %slice.375), channel_id=1, source_target_pairs={{0,1},{1,0},{2,3},{3,2},{4,5},{5,4},{6,7},{7,6},{8,9},{9,8},{10,11... | collective-permute-start | bytes 49160 | tf_op jit(solution)/shard_map/ppermute | solution.py:38
  328.0 3.9 %collective-permute-start.23 = (bf16[16,144,128]{2,1,0:T(8,128)(2,1)S(1)}, bf16[16,144,128]{2,1,0:T(8,128)(2,1)S(1)}, u32[]{:S(2)}, u32[]{:S(2)}) collective-permute-start(bf16[16,144,128]{2,1,0:T(8,128)(2,1)S(1)} %slice.244), channel_id=1, source_target_pairs={{0,2},{2,0},{4,6},{6,4},{8,10},{10,8},{12,14},{14,12},{16,18},{18,... | collective-permute-start | bytes 1769480 | tf_op jit(solution)/shard_map/ppermute | solution.py:43
  329.3 6.3 %collective-permute-start.28 = (bf16[16,144,128]{2,1,0:T(8,128)(2,1)S(1)}, bf16[16,144,128]{2,1,0:T(8,128)(2,1)S(1)}, u32[]{:S(2)}, u32[]{:S(2)}) collective-permute-start(bf16[16,144,128]{2,1,0:T(8,128)(2,1)S(1)} %slice.254), channel_id=1, source_target_pairs={{0,2},{2,0},{4,6},{6,4},{8,10},{10,8},{12,14},{14,12},{16,18},{18,... | collective-permute-start | bytes 1769480 | tf_op jit(solution)/shard_map/ppermute | solution.py:43
  333.2 23.4 %collective-permute-start.24 = (bf16[8,144,128]{2,1,0:T(8,128)(2,1)S(1)}, bf16[8,144,128]{2,1,0:T(8,128)(2,1)S(1)}, u32[]{:S(2)}, u32[]{:S(2)}) collective-permute-start(bf16[8,144,128]{2,1,0:T(8,128)(2,1)S(1)} %slice.364), channel_id=1, source_target_pairs={{0,16},{2,18},{4,20},{6,22},{8,24},{10,26},{12,28},{14,30},{16,0},... | collective-permute-start | bytes 884744 | tf_op jit(solution)/shard_map/ppermute | solution.py:43
  335.8 26.2 %collective-permute-start.29 = (bf16[8,144,128]{2,1,0:T(8,128)(2,1)S(1)}, bf16[8,144,128]{2,1,0:T(8,128)(2,1)S(1)}, u32[]{:S(2)}, u32[]{:S(2)}) collective-permute-start(bf16[8,144,128]{2,1,0:T(8,128)(2,1)S(1)} %slice.363), channel_id=1, source_target_pairs={{0,16},{2,18},{4,20},{6,22},{8,24},{10,26},{12,28},{14,30},{16,0},... | collective-permute-start | bytes 884744 | tf_op jit(solution)/shard_map/ppermute | solution.py:43
  336.8 25.3 %copy-start.32 = (bf16[4,32,32,128]{3,2,1,0:T(8,128)(2,1)}, bf16[4,32,32,128]{3,2,1,0:T(8,128)(2,1)S(1)}, u32[]{:S(2)}) copy-start(bf16[4,32,32,128]{3,2,1,0:T(8,128)(2,1)S(1)} %constant_dynamic-update-slice_fusion.45) | copy-start | bytes 3145732
  356.7 7.1 %collective-permute-start.25 = (bf16[4,144,128]{2,1,0:T(8,128)(2,1)S(1)}, bf16[4,144,128]{2,1,0:T(8,128)(2,1)S(1)}, u32[]{:S(2)}, u32[]{:S(2)}) collective-permute-start(bf16[4,144,128]{2,1,0:T(8,128)(2,1)S(1)} %slice.366), channel_id=1, source_target_pairs={{0,4},{2,6},{4,0},{6,2},{8,12},{10,14},{12,8},{14,10},{16,20},{18,... | collective-permute-start | bytes 442376 | tf_op jit(solution)/shard_map/ppermute | solution.py:43
  362.2 5.7 %collective-permute-start.30 = (bf16[4,144,128]{2,1,0:T(8,128)(2,1)S(1)}, bf16[4,144,128]{2,1,0:T(8,128)(2,1)S(1)}, u32[]{:S(2)}, u32[]{:S(2)}) collective-permute-start(bf16[4,144,128]{2,1,0:T(8,128)(2,1)S(1)} %slice.365), channel_id=1, source_target_pairs={{0,4},{2,6},{4,0},{6,2},{8,12},{10,14},{12,8},{14,10},{16,20},{18,... | collective-permute-start | bytes 442376 | tf_op jit(solution)/shard_map/ppermute | solution.py:43
  363.9 12.5 %copy-start.8 = (f32[128,144]{0,1:T(8,128)S(1)}, f32[128,144]{0,1:T(8,128)}, u32[]{:S(2)}) copy-start(f32[128,144]{0,1:T(8,128)} %param.33) | copy-start | bytes 221188
  363.9 12.5 %copy-start.15 = (f32[128,144]{0,1:T(8,128)S(1)}, f32[128,144]{0,1:T(8,128)}, u32[]{:S(2)}) copy-start(f32[128,144]{0,1:T(8,128)} %param.40) | copy-start | bytes 221188
  363.9 12.5 %copy-start.16 = (f32[128,144]{0,1:T(8,128)S(1)}, f32[128,144]{0,1:T(8,128)}, u32[]{:S(2)}) copy-start(f32[128,144]{0,1:T(8,128)} %param.41) | copy-start | bytes 221188
  363.9 4.4 %collective-permute-start.26 = (bf16[2,144,128]{2,1,0:T(8,128)(2,1)S(1)}, bf16[2,144,128]{2,1,0:T(8,128)(2,1)S(1)}, u32[]{:S(2)}, u32[]{:S(2)}) collective-permute-start(bf16[2,144,128]{2,1,0:T(8,128)(2,1)S(1)} %slice.369), channel_id=1, source_target_pairs={{0,8},{2,10},{4,12},{6,14},{8,0},{10,2},{12,4},{14,6},{16,24},{18,... | collective-permute-start | bytes 221192 | tf_op jit(solution)/shard_map/ppermute | solution.py:43
  367.9 4.4 %collective-permute-start.31 = (bf16[2,144,128]{2,1,0:T(8,128)(2,1)S(1)}, bf16[2,144,128]{2,1,0:T(8,128)(2,1)S(1)}, u32[]{:S(2)}, u32[]{:S(2)}) collective-permute-start(bf16[2,144,128]{2,1,0:T(8,128)(2,1)S(1)} %slice.368), channel_id=1, source_target_pairs={{0,8},{2,10},{4,12},{6,14},{8,0},{10,2},{12,4},{14,6},{16,24},{18,... | collective-permute-start | bytes 221192 | tf_op jit(solution)/shard_map/ppermute | solution.py:43
  368.4 4.8 %collective-permute-start.27 = (bf16[1,144,128]{2,1,0:T(8,128)(2,1)S(1)}, bf16[1,144,128]{2,1,0:T(8,128)(2,1)S(1)}, u32[]{:S(2)}, u32[]{:S(2)}) collective-permute-start(bf16[1,144,128]{2,1,0:T(8,128)(2,1)S(1)} %slice.372), channel_id=1, source_target_pairs={{0,1},{1,0},{2,3},{3,2},{4,5},{5,4},{6,7},{7,6},{8,9},{9,8},{10,11... | collective-permute-start | bytes 110600 | tf_op jit(solution)/shard_map/ppermute | solution.py:38
  372.4 4.0 %collective-permute-start.32 = (bf16[1,144,128]{2,1,0:T(8,128)(2,1)S(1)}, bf16[1,144,128]{2,1,0:T(8,128)(2,1)S(1)}, u32[]{:S(2)}, u32[]{:S(2)}) collective-permute-start(bf16[1,144,128]{2,1,0:T(8,128)(2,1)S(1)} %slice.371), channel_id=1, source_target_pairs={{0,1},{1,0},{2,3},{3,2},{4,5},{5,4},{6,7},{7,6},{8,9},{9,8},{10,11... | collective-permute-start | bytes 110600 | tf_op jit(solution)/shard_map/ppermute | solution.py:38
  (27 other events, 158.9 us)
